TPU v7x, 32 devices: a whole 2x2x4 slice. The times are simulated.
32 devices in a mesh: band: 4 (over y, core), grid: 8 (over z, x).
Axes of the slice: x: 2, y: 2, z: 4, core: 2. Of those that a mesh axis runs over, the one named last changes fastest.
Arguments:
- ground: float32 [4, 128, 128, 128], P('band', 'grid'), may hold values from -6 to 6
- response: float32 [4, 2, 2, 128, 128, 128], P('band', None, None, None, 'grid'), may hold values from -0.6 to 0.6
- kernel_xc: float32 [128, 128, 128], P('grid'), may hold values from -2 to -0.3
Outputs:
- applied: float32 [4, 2, 2, 128, 128, 128], P('band', None, None, None, 'grid')
All inputs are finite; a program needn't handle non-finite values.
Results may differ from a plain program's by a relative error of at most 0.0001.
Values sent between devices are 32-bit elements; how exact they have to be, the bound alone decides.
A program may use at most 64 MiB of HBM per device.

v0:
```python
import math

import jax
import jax.numpy as jnp
from jax import lax
from jax.sharding import PartitionSpec as P

highest = lax.Precision.HIGHEST
spacing = 0.4527
einsum_forms = ("...xyz,xk->...kyz", "...xyz,yk->...xkz", "...xyz,zk->...xyk")


def dft_tables(length):
    positions = jnp.arange(length, dtype=jnp.int32)
    phases = positions[:, None] * positions[None, :] % length
    angles = phases.astype(jnp.float32) * (2.0 * math.pi / length)
    factor = 1.0 / math.sqrt(length)
    return (jnp.cos(angles) * factor, jnp.sin(angles) * factor)


def along(complex_pair, which_axis, tables, direction):
    real_part, imag_part = complex_pair
    cosine, sine_part = tables

    def contract(operand, matrix):
        return jnp.einsum(einsum_forms[which_axis], operand, matrix, precision=highest)

    new_real = contract(real_part, cosine) - direction * contract(imag_part, sine_part)
    new_imag = contract(imag_part, cosine) + direction * contract(real_part, sine_part)
    return (new_real, new_imag)


def signed_freq(positions, length):
    return jnp.where(positions < (length + 1) // 2, positions, positions - length).astype(
        jnp.float32
    )


def coulomb(freq_first, freq_second, freq_third, length):
    squares = (
        freq_first[:, None, None] ** 2
        + freq_second[None, :, None] ** 2
        + freq_third[None, None, :] ** 2
    )
    edge_len = spacing * length
    return jnp.where(
        squares > 0.5, edge_len * edge_len / (math.pi * jnp.maximum(squares, 1.0)), 0.0
    )


def scaled(complex_pair, weights):
    return (complex_pair[0] * weights, complex_pair[1] * weights)


def potential_whole(density, kernel_xc, tables, grid_len):
    wave_values = along(along(density, 1, tables, -1.0), 2, tables, -1.0)
    wave_values = (
        lax.all_to_all(wave_values[0], "grid", split_axis=1, concat_axis=0, tiled=True),
        lax.all_to_all(wave_values[1], "grid", split_axis=1, concat_axis=0, tiled=True),
    )
    wave_values = along(wave_values, 0, tables, -1.0)
    row_count = wave_values[0].shape[1]
    positions = jnp.arange(grid_len, dtype=jnp.int32)
    freq_second = signed_freq(
        lax.axis_index("grid") * row_count + jnp.arange(row_count, dtype=jnp.int32), grid_len
    )
    weights = coulomb(
        signed_freq(positions, grid_len), freq_second, signed_freq(positions, grid_len), grid_len
    )
    wave_values = along(scaled(wave_values, weights), 0, tables, 1.0)
    cell_values = (
        lax.all_to_all(wave_values[0], "grid", split_axis=0, concat_axis=1, tiled=True),
        lax.all_to_all(wave_values[1], "grid", split_axis=0, concat_axis=1, tiled=True),
    )
    cell_values = along(along(cell_values, 1, tables, 1.0), 2, tables, 1.0)
    return (cell_values[0] + kernel_xc * density[0], cell_values[1] + kernel_xc * density[1])


def on_device(ground, response, kernel_xc):
    grid_len = ground.shape[2]
    tables = dft_tables(grid_len)
    wave_values = (response[:, :, 0], response[:, :, 1])
    wave_values = along(along(wave_values, 0, tables, 1.0), 2, tables, 1.0)
    cell_values = (
        lax.all_to_all(wave_values[0], "grid", split_axis=2, concat_axis=3, tiled=True),
        lax.all_to_all(wave_values[1], "grid", split_axis=2, concat_axis=3, tiled=True),
    )
    cell_values = along(cell_values, 1, tables, 1.0)
    dens_real = jnp.sum(ground * (cell_values[0][:, 0] + cell_values[0][:, 1]), axis=0)
    dens_imag = jnp.sum(ground * (cell_values[1][:, 0] - cell_values[1][:, 1]), axis=0)
    density = lax.psum((dens_real, dens_imag), "band")
    pot_real, pot_imag = potential_whole(density, kernel_xc, tables, grid_len)
    prod_real = ground * pot_real
    prod_imag = ground * pot_imag
    fields = (jnp.stack((prod_real, prod_real), axis=1), jnp.stack((prod_imag, -prod_imag), axis=1))
    fields = along(along(fields, 1, tables, -1.0), 2, tables, -1.0)
    wave_out = (
        lax.all_to_all(fields[0], "grid", split_axis=3, concat_axis=2, tiled=True),
        lax.all_to_all(fields[1], "grid", split_axis=3, concat_axis=2, tiled=True),
    )
    wave_out = along(wave_out, 0, tables, -1.0)
    return jnp.stack(wave_out, axis=2)


def solution(mesh):
    return jax.shard_map(
        on_device,
        mesh=mesh,
        in_specs=(
            P("band", "grid", None, None),
            P("band", None, None, None, "grid", None),
            P("grid", None, None),
        ),
        out_specs=P("band", None, None, None, "grid", None),
        check_vma=False,
    )
```

profile of v0, /device:TPU:0, one launch (start us, length us, event | category | flops | bytes accessed | tf_op | source)
XLA Modules:
  0.0 492.5 jit_solution(3142891739396519265)
XLA Ops:
  6.5 2.5 fusion.380
  9.1 2.6 fusion.18
  11.7 2.6 fusion.19
  14.3 2.6 fusion.25
  16.9 2.6 fusion.24
  19.5 2.4 fusion.12
  24.0 2.5 copy.35
  26.6 7.3 %all-to-all-start = ((f32[1,2,128,16,128]{4,3,1,0,2:T(8,128)}), f32[1,2,128,16,128]{4,3,1,0,2:T(8,128)}, u32[]{:S(2)}, u32[]{:S(2)}) async-start(f32[1,2,128,16,128]{4,3,1,0,2:T(8,128)} %copy.35), calls=%async_computation | async-start | bytes 4194304 | tf_op jit(solution)/shard_map/all_to_all | solution.py:85
  33.8 3.7 fusion.10
  39.7 2.5 copy.39
  42.2 40.0 %all-to-all-done = f32[1,2,128,16,128]{4,3,1,0,2:T(8,128)} async-done(((f32[1,2,128,16,128]{4,3,1,0,2:T(8,128)}), f32[1,2,128,16,128]{4,3,1,0,2:T(8,128)}, u32[]{:S(2)}, u32[]{:S(2)}) %all-to-all-start) | async-done | bytes 2097184 | tf_op jit(solution)/shard_map/all_to_all | solution.py:85
  82.2 4.4 all-to-all-start.1
  88.8 45.5 %all-to-all-done.1 = f32[1,2,128,16,128]{4,3,1,0,2:T(8,128)} async-done(((f32[1,2,128,16,128]{4,3,1,0,2:T(8,128)}), f32[1,2,128,16,128]{4,3,1,0,2:T(8,128)}, u32[]{:S(2)}, u32[]{:S(2)}) %all-to-all-start.1) | async-done | bytes 2097184 | tf_op jit(solution)/shard_map/all_to_all | solution.py:86
  146.8 50.8 %all-reduce.3.cloned.1.call-done = (f32[16,128,128]{2,1,0:T(8,128)}, f32[16,128,128]{2,1,0:T(8,128)}) async-done(((f32[16,128,128]{2,1,0:T(8,128)}, f32[16,128,128]{2,1,0:T(8,128)}), (f32[16,128,128]{2,1,0:T(8,128)}, f32[16,128,128]{2,1,0:T(8,128)})) %all-reduce.3.cloned.1.call-update) | async-done | bytes 2097168 | tf_op jit(solution)/shard_map/psum | solution.py:91
  197.6 2.6 fusion.111
  208.4 5.5 %all-to-all-start.2 = ((f32[16,128,128]{2,0,1:T(8,128)}), f32[16,128,128]{2,0,1:T(8,128)}, u32[]{:S(2)}, u32[]{:S(2)}) async-start(f32[16,128,128]{2,0,1:T(8,128)} %copy.43), calls=%async_computation.2 | async-start | bytes 2097152 | tf_op jit(solution)/shard_map/all_to_all | solution.py:58
  218.0 21.8 %all-to-all-done.2 = f32[16,128,128]{2,0,1:T(8,128)} async-done(((f32[16,128,128]{2,0,1:T(8,128)}), f32[16,128,128]{2,0,1:T(8,128)}, u32[]{:S(2)}, u32[]{:S(2)}) %all-to-all-start.2) | async-done | bytes 1048608 | tf_op jit(solution)/shard_map/all_to_all | solution.py:58
  239.7 3.8 all-to-all-start.3
  245.0 24.5 %all-to-all-done.3 = f32[16,128,128]{2,0,1:T(8,128)S(1)} async-done(((f32[16,128,128]{2,0,1:T(8,128)}), f32[16,128,128]{2,0,1:T(8,128)S(1)}, u32[]{:S(2)}, u32[]{:S(2)}) %all-to-all-start.3) | async-done | bytes 1048608 | tf_op jit(solution)/shard_map/all_to_all | solution.py:59
  279.3 4.2 all-to-all-start.4
  287.7 21.5 %all-to-all-done.4 = f32[128,16,128]{2,1,0:T(8,128)} async-done(((f32[128,16,128]{2,1,0:T(8,128)}), f32[128,16,128]{2,1,0:T(8,128)}, u32[]{:S(2)}, u32[]{:S(2)}) %all-to-all-start.4) | async-done | bytes 1048608 | tf_op jit(solution)/shard_map/all_to_all | solution.py:72
  309.2 4.0 all-to-all-start.5
  314.5 24.0 %all-to-all-done.5 = f32[128,16,128]{2,1,0:T(8,128)S(1)} async-done(((f32[128,16,128]{2,1,0:T(8,128)}), f32[128,16,128]{2,1,0:T(8,128)S(1)}, u32[]{:S(2)}, u32[]{:S(2)}) %all-to-all-start.5) | async-done | bytes 1048608 | tf_op jit(solution)/shard_map/all_to_all | solution.py:73
  362.5 2.7 copy.59
  365.2 4.4 all-to-all-start.6
  369.6 3.7 fusion.2
  375.5 2.5 copy.63
  378.0 39.4 %all-to-all-done.6 = f32[1,2,16,128,128]{4,2,1,0,3:T(8,128)} async-done(((f32[1,2,16,128,128]{4,2,1,0,3:T(8,128)}), f32[1,2,16,128,128]{4,2,1,0,3:T(8,128)}, u32[]{:S(2)}, u32[]{:S(2)}) %all-to-all-start.6) | async-done | bytes 2097184 | tf_op jit(solution)/shard_map/all_to_all | solution.py:98
  417.4 4.4 all-to-all-start.7
  423.6 45.9 %all-to-all-done.7 = f32[1,2,16,128,128]{4,2,1,0,3:T(8,128)} async-done(((f32[1,2,16,128,128]{4,2,1,0,3:T(8,128)}), f32[1,2,16,128,128]{4,2,1,0,3:T(8,128)}, u32[]{:S(2)}, u32[]{:S(2)}) %all-to-all-start.7) | async-done | bytes 2097184 | tf_op jit(solution)/shard_map/all_to_all | solution.py:99
  478.0 2.3 subtract_bitcast_fusion
  480.8 4.4 copy.65
  (75 shorter events, 84.5 us)
Async XLA Ops:
  19.5 2.4 copy-start.1
  26.6 55.6 %all-to-all-start = ((f32[1,2,128,16,128]{4,3,1,0,2:T(8,128)}), f32[1,2,128,16,128]{4,3,1,0,2:T(8,128)}, u32[]{:S(2)}, u32[]{:S(2)}) async-start(f32[1,2,128,16,128]{4,3,1,0,2:T(8,128)} %copy.35), calls=%async_computation | async-start | bytes 4194304 | tf_op jit(solution)/shard_map/all_to_all | solution.py:85
  82.2 52.2 %all-to-all-start.1 = ((f32[1,2,128,16,128]{4,3,1,0,2:T(8,128)}), f32[1,2,128,16,128]{4,3,1,0,2:T(8,128)}, u32[]{:S(2)}, u32[]{:S(2)}) async-start(f32[1,2,128,16,128]{4,3,1,0,2:T(8,128)} %copy.39), calls=%async_computation.1 | async-start | bytes 4194304 | tf_op jit(solution)/shard_map/all_to_all | solution.py:86
  86.5 111.1 %all-reduce.3.cloned.1.call-start = ((), (), s32[]{:S(2)}) async-start(), calls=%async_computation.8 | async-start | bytes 4194304 | tf_op jit(solution)/shard_map/psum | solution.py:91
  142.7 2.3 copy-start.5
  197.6 2.6 copy-start.2
  201.5 2.7 copy-start.3
  208.4 31.3 %all-to-all-start.2 = ((f32[16,128,128]{2,0,1:T(8,128)}), f32[16,128,128]{2,0,1:T(8,128)}, u32[]{:S(2)}, u32[]{:S(2)}) async-start(f32[16,128,128]{2,0,1:T(8,128)} %copy.43), calls=%async_computation.2 | async-start | bytes 2097152 | tf_op jit(solution)/shard_map/all_to_all | solution.py:58
  239.7 29.7 %all-to-all-start.3 = ((f32[16,128,128]{2,0,1:T(8,128)}), f32[16,128,128]{2,0,1:T(8,128)S(1)}, u32[]{:S(2)}, u32[]{:S(2)}) async-start(f32[16,128,128]{2,0,1:T(8,128)} %copy.47), calls=%async_computation.3 | async-start | bytes 2097152 | tf_op jit(solution)/shard_map/all_to_all | solution.py:59
  279.3 29.9 %all-to-all-start.4 = ((f32[128,16,128]{2,1,0:T(8,128)}), f32[128,16,128]{2,1,0:T(8,128)}, u32[]{:S(2)}, u32[]{:S(2)}) async-start(f32[128,16,128]{2,1,0:T(8,128)} %copy.49), calls=%async_computation.4 | async-start | bytes 2097152 | tf_op jit(solution)/shard_map/all_to_all | solution.py:72
  309.2 29.4 %all-to-all-start.5 = ((f32[128,16,128]{2,1,0:T(8,128)}), f32[128,16,128]{2,1,0:T(8,128)S(1)}, u32[]{:S(2)}, u32[]{:S(2)}) async-start(f32[128,16,128]{2,1,0:T(8,128)} %copy.51), calls=%async_computation.5 | async-start | bytes 2097152 | tf_op jit(solution)/shard_map/all_to_all | solution.py:73
  343.8 2.5 copy-start.4
  343.9 2.5 copy-start.6
  343.9 2.5 copy-start.7
  358.2 2.2 copy-start
  365.2 52.2 %all-to-all-start.6 = ((f32[1,2,16,128,128]{4,2,1,0,3:T(8,128)}), f32[1,2,16,128,128]{4,2,1,0,3:T(8,128)}, u32[]{:S(2)}, u32[]{:S(2)}) async-start(f32[1,2,16,128,128]{4,2,1,0,3:T(8,128)} %copy.59), calls=%async_computation.6 | async-start | bytes 4194304 | tf_op jit(solution)/shard_map/all_to_all | solution.py:98
  417.4 52.2 %all-to-all-start.7 = ((f32[1,2,16,128,128]{4,2,1,0,3:T(8,128)}), f32[1,2,16,128,128]{4,2,1,0,3:T(8,128)}, u32[]{:S(2)}, u32[]{:S(2)}) async-start(f32[1,2,16,128,128]{4,2,1,0,3:T(8,128)} %copy.63), calls=%async_computation.7 | async-start | bytes 4194304 | tf_op jit(solution)/shard_map/all_to_all | solution.py:99
Sparse Core Ops, SparseCore 0:
  146.9 50.6 all-reduce.2
where the time goes:
time: 502 us; the launch traced here: 492 us
  waiting for transfers between devices  313 us (62%)
  matrix products  90.1 us (18%)
  starting transfers between devices  38.3 us (8%)
  local copies, waits for them, and re-layouts  33.9 us (7%)
  between operations  14.4 us (3%)
    dot_general x48, matrix products, contract(): jnp.einsum(einsum_forms[which_axis], operand, matrix, precision=highest)  90.1 us
    psum x1, waiting for transfers between devices, on_device(): density = lax.psum((dens_real, dens_imag), 'band')  50.8 us
    all_to_all x1, waiting for transfers between devices, on_device(): lax.all_to_all(fields[1], 'grid', split_axis=3, concat_axis=2, tiled=True)  45.9 us
    all_to_all x1, waiting for transfers between devices, on_device(): lax.all_to_all(wave_values[1], 'grid', split_axis=2, concat_axis=3, tiled...  45.5 us
    all_to_all x1, waiting for transfers between devices, on_device(): lax.all_to_all(wave_values[0], 'grid', split_axis=2, concat_axis=3, tiled...  40 us
    all_to_all x1, waiting for transfers between devices, on_device(): lax.all_to_all(fields[0], 'grid', split_axis=3, concat_axis=2, tiled=True)  39.4 us
    all_to_all x1, waiting for transfers between devices, potential_whole(): lax.all_to_all(wave_values[1], 'grid', split_axis=1, concat_axis=0, tiled...  24.5 us
    all_to_all x1, waiting for transfers between devices, potential_whole(): lax.all_to_all(wave_values[1], 'grid', split_axis=0, concat_axis=1, tiled...  24 us
  transfers between devices with their start and end apart: 9, of which 9 were waited for; matrix products, arithmetic and copies ran while one was open for 6% of the time, Pallas kernels for 0%

commit v1 on v0

v1 whole, which is shorter than its diff:
```python
import math

import jax
import jax.numpy as jnp
import numpy as np
from jax import lax
from jax.sharding import PartitionSpec as P

high = lax.Precision.HIGH
spacing = 0.4527


def dft_pair(length, direction, rows=None, columns=None):
    rows = np.arange(length) if rows is None else rows
    columns = np.arange(length) if columns is None else columns
    angles = (rows[:, None] * columns[None, :] % length) * (2.0 * math.pi / length)
    cosine = np.cos(angles) / math.sqrt(length)
    sine = direction * np.sin(angles) / math.sqrt(length)
    pairs = (np.stack((cosine, sine), axis=1), np.stack((-sine, cosine), axis=1))
    return np.stack(pairs, axis=0).astype(np.float32)


def ein(form, operand, table):
    return jnp.einsum(form, operand, table, precision=high)


def signed_freq(positions, length):
    return jnp.where(positions < (length + 1) // 2, positions, positions - length).astype(
        jnp.float32
    )


def coulomb(freq_first, freq_second, freq_third, length):
    squares = (
        freq_first[:, None, None] ** 2
        + freq_second[None, :, None] ** 2
        + freq_third[None, None, :] ** 2
    )
    edge_len = spacing * length
    return jnp.where(
        squares > 0.5, edge_len * edge_len / (math.pi * jnp.maximum(squares, 1.0)), 0.0
    )


def swap(values, bit, size):
    return lax.ppermute(values, "band", [(i, i ^ bit) for i in range(size)])


def hartree(density, axes, device, devices, numbers):
    length = density.shape[-1]
    forward, backward = dft_pair(length, -1.0), dft_pair(length, 1.0)
    wave = ein("cxyz,cydk->dxkz", density, forward)
    wave = ein("dxkz,dzem->exkm", wave, forward)
    wave = lax.all_to_all(wave, axes, split_axis=2, concat_axis=1, tiled=True)
    rows = length // devices
    mine = device * rows + jnp.arange(rows, dtype=jnp.int32)
    freqs = signed_freq(jnp.arange(length, dtype=jnp.int32), length)
    weights = coulomb(freqs, signed_freq(mine, length), freqs, length)
    wave = ein("cxyz,cxdk->dkyz", wave, dft_pair(length, -1.0, rows=numbers)) * weights
    wave = ein("dkyz,dkex->exyz", wave, dft_pair(length, 1.0, columns=numbers))
    wave = lax.all_to_all(wave, axes, split_axis=1, concat_axis=2, tiled=True)
    cell = ein("dxkz,dzem->exkm", wave, backward)
    return ein("cxyz,cydk->dxkz", cell, backward)


def on_device(bands, grids, ground, response, kernel_xc):
    grid_len = ground.shape[2]
    planes = ground.shape[1]
    forward = dft_pair(grid_len, -1.0)
    backward = dft_pair(grid_len, 1.0)
    orbital = ground[0]

    flip = np.array([1.0, -1.0], np.float32)[None, None, :, None]
    partial = None
    for harmonic in range(2):
        table = backward if harmonic == 0 else backward * flip
        wave = ein("cxyz,cxdk->dkyz", response[0, harmonic], backward)
        wave = lax.all_to_all(wave, "grid", split_axis=1, concat_axis=2, tiled=True)
        wave = ein("dxkz,dzem->exkm", wave, backward)
        cell = ein("cxyz,cydk->dxkz", wave, table)
        partial = cell if partial is None else partial + cell
    partial = partial * orbital

    me_band = lax.axis_index("band")
    if planes % bands == 0 and bands & (bands - 1) == 0:
        dens = partial
        kernel = kernel_xc
        bit = bands // 2
        bits = []
        while bit >= 1:
            bits.append(bit)
            bit //= 2
        steps = list(reversed(bits))
        low = jnp.int32(0)
        for bit in steps:
            half = dens.shape[1] // 2
            mine = (me_band // bit) % 2
            keep = lax.dynamic_slice_in_dim(dens, mine * half, half, 1)
            give = lax.dynamic_slice_in_dim(dens, (1 - mine) * half, half, 1)
            dens = keep + swap(give, bit, bands)
            low = low + mine * half
        own = dens.shape[1]
        kernel = lax.dynamic_slice_in_dim(kernel_xc, low, own, 0)
        place = [0] * bands
        for b in range(bands):
            size = planes
            for bit in steps:
                size //= 2
                place[b] += ((b // bit) % 2) * (size // own)
        numbers = (
            np.arange(grids)[None, :, None] * planes
            + np.array(place)[:, None, None] * own
            + np.arange(own)[None, None, :]
        ).reshape(-1)
        device = me_band * grids + lax.axis_index("grid")
        pot = hartree(dens, ("band", "grid"), device, bands * grids, numbers)
        pot = pot + kernel * dens
        for bit in reversed(steps):
            mine = (me_band // bit) % 2
            other = swap(pot, bit, bands)
            first = jnp.where(mine == 0, pot, other)
            second = jnp.where(mine == 0, other, pot)
            pot = jnp.concatenate((first, second), axis=1)
    else:
        dens = lax.psum(partial, "band")
        pot = hartree(dens, "grid", lax.axis_index("grid"), grids, None)
        pot = pot + kernel_xc * dens

    prod = pot * orbital
    outs = []
    for harmonic in range(2):
        table = forward if harmonic == 0 else forward * flip.reshape(2, 1, 1, 1)
        wave = ein("cxyz,cydk->dxkz", prod, table)
        wave = ein("dxkz,dzem->exkm", wave, forward)
        wave = lax.all_to_all(wave, "grid", split_axis=2, concat_axis=1, tiled=True)
        outs.append(ein("cxyz,cxdk->dkyz", wave, forward))
    return jnp.stack(outs, axis=0)[None]


def solution(mesh):
    bands, grids = mesh.shape["band"], mesh.shape["grid"]

    def body(ground, response, kernel_xc):
        return on_device(bands, grids, ground, response, kernel_xc)

    return jax.shard_map(
        body,
        mesh=mesh,
        in_specs=(
            P("band", "grid", None, None),
            P("band", None, None, None, "grid", None),
            P("grid", None, None),
        ),
        out_specs=P("band", None, None, None, "grid", None),
        check_vma=False,
    )
```

time: 502 us -> 337 us (0.67)
  the two profiles are of different devices: /device:TPU:0 before, /device:TPU:10 now
where the time goes in v1:
time: 337 us; the launch traced here: 331 us
  waiting for transfers between devices  216 us (64%)
  starting transfers between devices  43.7 us (13%)
  local copies, waits for them, and re-layouts  39.6 us (12%)
  matrix products  25.6 us (8%)
  other arithmetic  5.86 us (2%)
    all_to_all x2, waiting for transfers between devices, on_device(): wave = lax.all_to_all(wave, 'grid', split_axis=2, concat_axis=1, tiled=True)  81.7 us
    all_to_all x2, waiting for transfers between devices, on_device(): wave = lax.all_to_all(wave, 'grid', split_axis=1, concat_axis=2, tiled=True)  80.2 us
    ppermute x4, waiting for transfers between devices, swap(): return lax.ppermute(values, 'band', [(i, i ^ bit) for i in range(size)])  30 us
    dot_general x18, matrix products, ein(): return jnp.einsum(form, operand, table, precision=high)  25.6 us
    all_to_all x2, starting transfers between devices, on_device(): wave = lax.all_to_all(wave, 'grid', split_axis=1, concat_axis=2, tiled=True)  13.8 us
    all_to_all x2, starting transfers between devices, on_device(): wave = lax.all_to_all(wave, 'grid', split_axis=2, concat_axis=1, tiled=True)  13.6 us
    all_to_all x1, waiting for transfers between devices, hartree(): wave = lax.all_to_all(wave, axes, split_axis=2, concat_axis=1, tiled=True)  12.5 us
    all_to_all x1, waiting for transfers between devices, hartree(): wave = lax.all_to_all(wave, axes, split_axis=1, concat_axis=2, tiled=True)  11.7 us
  transfers between devices with their start and end apart: 10, of which 10 were waited for; matrix products, arithmetic and copies ran while one was open for 6% of the time, Pallas kernels for 0%

profile of v1, /device:TPU:10, one launch (start us, length us, event | category | flops | bytes accessed | tf_op | source)
XLA Modules:
  0.0 331.2 jit_solution(17473547233296567763)
XLA Ops:
  0.0 4.0 %fusion.46 = (f32[1,1,2,128,16,128]{5,4,3,2,1,0:T(8,128)S(1)}, f32[1,1,2,128,16,128]{5,4,3,2,1,0:T(8,128)}) fusion(f32[1,2,2,128,16,128]{5,4,3,2,1,0:T(8,128)} %param.22), kind=kLoop, calls=%fused_computation.68 | loop fusion | bytes 8388608 | tf_op jit(solution)/shard_map/slice | solution.py:77
  5.7 2.5 copy.81
  8.2 6.2 %all-to-all-start = ((f32[2,128,16,128]{3,2,0,1:T(8,128)}), f32[2,128,16,128]{3,2,0,1:T(8,128)}, u32[]{:S(2)}, u32[]{:S(2)}) async-start(f32[2,128,16,128]{3,2,0,1:T(8,128)} %copy.81), calls=%async_computation | async-start | bytes 4194304 | tf_op jit(solution)/shard_map/all_to_all | solution.py:78
  14.4 3.2 fusion.24
  17.6 2.5 copy.89
  20.2 39.2 %all-to-all-done = f32[2,128,16,128]{3,2,0,1:T(8,128)} async-done(((f32[2,128,16,128]{3,2,0,1:T(8,128)}), f32[2,128,16,128]{3,2,0,1:T(8,128)}, u32[]{:S(2)}, u32[]{:S(2)}) %all-to-all-start) | async-done | bytes 2097184 | tf_op jit(solution)/shard_map/all_to_all | solution.py:78
  59.4 7.6 %all-to-all-start.1 = ((f32[2,128,16,128]{3,2,0,1:T(8,128)}), f32[2,128,16,128]{3,2,0,1:T(8,128)}, u32[]{:S(2)}, u32[]{:S(2)}) async-start(f32[2,128,16,128]{3,2,0,1:T(8,128)} %copy.89), calls=%async_computation.1 | async-start | bytes 4194304 | tf_op jit(solution)/shard_map/all_to_all | solution.py:78
  67.4 3.2 copy.83
  70.6 41.0 %all-to-all-done.1 = f32[2,128,16,128]{3,2,0,1:T(8,128)} async-done(((f32[2,128,16,128]{3,2,0,1:T(8,128)}), f32[2,128,16,128]{3,2,0,1:T(8,128)}, u32[]{:S(2)}, u32[]{:S(2)}) %all-to-all-start.1) | async-done | bytes 2097184 | tf_op jit(solution)/shard_map/all_to_all | solution.py:78
  111.6 2.0 copy.91
  115.9 1.9 fusion.7
  117.7 1.9 bitcast_multiply_fusion
  121.2 2.7 collective-permute-done
  128.0 12.8 %collective-permute-done.1 = f32[2,4,128,128]{2,3,0,1:T(8,128)} collective-permute-done((f32[2,4,128,128]{2,3,0,1:T(8,128)}, f32[2,4,128,128]{2,3,0,1:T(8,128)}, u32[]{:S(2)}, u32[]{:S(2)}) %collective-permute-start.1) | collective-permute-done | bytes 524320 | tf_op jit(solution)/shard_map/ppermute | solution.py:46
  144.0 6.9 %all-to-all-start.2 = ((f32[2,4,128,128]{3,0,1,2:T(2,128)}), f32[2,4,128,128]{3,0,1,2:T(2,128)}, u32[]{:S(2)}, u32[]{:S(2)}) async-start(f32[2,4,128,128]{3,0,1,2:T(2,128)} %copy.97), calls=%async_computation.2 | async-start | bytes 1048576 | tf_op jit(solution)/shard_map/all_to_all | solution.py:54
  151.8 12.5 %all-to-all-done.2 = f32[2,4,128,128]{3,0,1,2:T(2,128)} async-done(((f32[2,4,128,128]{3,0,1,2:T(2,128)}), f32[2,4,128,128]{3,0,1,2:T(2,128)}, u32[]{:S(2)}, u32[]{:S(2)}) %all-to-all-start.2) | async-done | bytes 524320 | tf_op jit(solution)/shard_map/all_to_all | solution.py:54
  168.5 6.1 %all-to-all-start.3 = ((f32[2,128,4,128]{3,2,0,1:T(4,128)}), f32[2,128,4,128]{3,2,0,1:T(4,128)}, u32[]{:S(2)}, u32[]{:S(2)}) async-start(f32[2,128,4,128]{3,2,0,1:T(4,128)} %copy.100), calls=%async_computation.3 | async-start | bytes 1048576 | tf_op jit(solution)/shard_map/all_to_all | solution.py:61
  176.5 11.7 %all-to-all-done.3 = f32[2,128,4,128]{3,2,0,1:T(4,128)} async-done(((f32[2,128,4,128]{3,2,0,1:T(4,128)}), f32[2,128,4,128]{3,2,0,1:T(4,128)}, u32[]{:S(2)}, u32[]{:S(2)}) %all-to-all-start.3) | async-done | bytes 524320 | tf_op jit(solution)/shard_map/all_to_all | solution.py:61
  190.7 1.7 multiply_add_fusion
  194.0 12.5 %collective-permute-done.2 = f32[2,4,128,128]{2,3,0,1:T(8,128)S(1)} collective-permute-done((f32[2,4,128,128]{2,3,0,1:T(8,128)S(1)}, f32[2,4,128,128]{2,3,0,1:T(8,128)S(1)}, u32[]{:S(2)}, u32[]{:S(2)}) %collective-permute-start.2) | collective-permute-done | bytes 524320 | tf_op jit(solution)/shard_map/ppermute | solution.py:46
  208.6 2.0 collective-permute-done.3
  210.6 1.7 broadcast_select_fusion.1
  213.3 1.9 fusion.20
  215.2 2.9 copy.112
  218.1 6.6 %all-to-all-start.5 = ((f32[2,16,128,128]{3,0,1,2:T(2,128)}), f32[2,16,128,128]{3,0,1,2:T(2,128)}, u32[]{:S(2)}, u32[]{:S(2)}) async-start(f32[2,16,128,128]{3,0,1,2:T(2,128)} %copy.112), calls=%async_computation.5 | async-start | bytes 4194304 | tf_op jit(solution)/shard_map/all_to_all | solution.py:135
  225.7 1.9 fusion.17
  227.6 2.9 copy.108
  230.5 39.7 %all-to-all-done.5 = f32[2,16,128,128]{3,0,1,2:T(2,128)} async-done(((f32[2,16,128,128]{3,0,1,2:T(2,128)}), f32[2,16,128,128]{3,0,1,2:T(2,128)}, u32[]{:S(2)}, u32[]{:S(2)}) %all-to-all-start.5) | async-done | bytes 2097184 | tf_op jit(solution)/shard_map/all_to_all | solution.py:135
  270.2 7.0 %all-to-all-start.4 = ((f32[2,16,128,128]{3,0,1,2:T(2,128)}), f32[2,16,128,128]{3,0,1,2:T(2,128)S(1)}, u32[]{:S(2)}, u32[]{:S(2)}) async-start(f32[2,16,128,128]{3,0,1,2:T(2,128)} %copy.108), calls=%async_computation.4 | async-start | bytes 4194304 | tf_op jit(solution)/shard_map/all_to_all | solution.py:135
  277.2 3.2 copy.113
  280.4 42.0 %all-to-all-done.4 = f32[2,16,128,128]{3,0,1,2:T(2,128)S(1)} async-done(((f32[2,16,128,128]{3,0,1,2:T(2,128)}), f32[2,16,128,128]{3,0,1,2:T(2,128)S(1)}, u32[]{:S(2)}, u32[]{:S(2)}) %all-to-all-start.4) | async-done | bytes 2097184 | tf_op jit(solution)/shard_map/all_to_all | solution.py:135
  326.8 4.4 %copy.115 = f32[1,2,2,128,16,128]{5,4,3,2,1,0:T(8,128)} copy(f32[1,2,2,128,16,128]{5,3,4,2,1,0:T(8,128)S(1)} %maximum_bitcast_fusion) | data formatting | bytes 8388608 | tf_op jit(solution)/shard_map/broadcast_in_dim | solution.py:137
  (68 shorter events, 32.4 us)
Async XLA Ops:
  0.0 174.7 %copy-start = (f32[16,128,128]{2,1,0:T(8,128)S(1)}, f32[16,128,128]{2,1,0:T(8,128)}, u32[]{:S(2)}) copy-start(f32[16,128,128]{2,1,0:T(8,128)} %param.23) | copy-start | bytes 3145732
  0.0 4.0 %copy-start.12 = (f32[2,128,2,128,1]{1,3,0,4,2:T(8,128)S(1)}, f32[2,128,2,128,1]{1,3,0,4,2:T(8,128)}, u32[]{:S(2)}) copy-start(f32[2,128,2,128,1]{1,3,0,4,2:T(8,128)} %constant.98) | copy-start | bytes 786436
  8.2 51.2 %all-to-all-start = ((f32[2,128,16,128]{3,2,0,1:T(8,128)}), f32[2,128,16,128]{3,2,0,1:T(8,128)}, u32[]{:S(2)}, u32[]{:S(2)}) async-start(f32[2,128,16,128]{3,2,0,1:T(8,128)} %copy.81), calls=%async_computation | async-start | bytes 4194304 | tf_op jit(solution)/shard_map/all_to_all | solution.py:78
  20.2 46.9 %copy-start.13 = (f32[1,16,128,128]{3,2,1,0:T(8,128)S(1)}, f32[1,16,128,128]{3,2,1,0:T(8,128)}, u32[]{:S(2)}) copy-start(f32[1,16,128,128]{3,2,1,0:T(8,128)} %param.21) | copy-start | bytes 3145732
  59.4 52.2 %all-to-all-start.1 = ((f32[2,128,16,128]{3,2,0,1:T(8,128)}), f32[2,128,16,128]{3,2,0,1:T(8,128)}, u32[]{:S(2)}, u32[]{:S(2)}) async-start(f32[2,128,16,128]{3,2,0,1:T(8,128)} %copy.89), calls=%async_computation.1 | async-start | bytes 4194304 | tf_op jit(solution)/shard_map/all_to_all | solution.py:78
  111.6 2.2 copy-start.2
  111.6 2.2 copy-start.6
  114.8 1.1 copy-start.14
  119.7 1.3 copy-start.4
  121.1 2.9 collective-permute-start
  121.2 19.5 %copy-start.5 = (f32[2,128,2,128,1]{3,1,0,2,4:T(8,128)S(1)}, f32[2,128,2,128,1]{3,1,0,2,4:T(8,128)}, u32[]{:S(2)}) copy-start(f32[2,128,2,128,1]{3,1,0,2,4:T(8,128)} %constant.101) | copy-start | bytes 786436
  126.5 14.3 %collective-permute-start.1 = (f32[2,4,128,128]{2,3,0,1:T(8,128)}, f32[2,4,128,128]{2,3,0,1:T(8,128)}, u32[]{:S(2)}, u32[]{:S(2)}) collective-permute-start(f32[2,4,128,128]{2,3,0,1:T(8,128)} %constant_dynamic-slice_fusion.1), channel_id=1, source_target_pairs={{0,16},{8,24},{16,0},{24,8},{1,17},{9,25},{17,1},{25,9},{2,18},{10... | collective-permute-start | bytes 1572872 | tf_op jit(solution)/shard_map/ppermute | solution.py:46
  144.0 20.4 %all-to-all-start.2 = ((f32[2,4,128,128]{3,0,1,2:T(2,128)}), f32[2,4,128,128]{3,0,1,2:T(2,128)}, u32[]{:S(2)}, u32[]{:S(2)}) async-start(f32[2,4,128,128]{3,0,1,2:T(2,128)} %copy.97), calls=%async_computation.2 | async-start | bytes 1048576 | tf_op jit(solution)/shard_map/all_to_all | solution.py:54
  164.3 2.7 copy-start.16
  168.5 19.7 %all-to-all-start.3 = ((f32[2,128,4,128]{3,2,0,1:T(4,128)}), f32[2,128,4,128]{3,2,0,1:T(4,128)}, u32[]{:S(2)}, u32[]{:S(2)}) async-start(f32[2,128,4,128]{3,2,0,1:T(4,128)} %copy.100), calls=%async_computation.3 | async-start | bytes 1048576 | tf_op jit(solution)/shard_map/all_to_all | solution.py:61
  175.4 15.3 %copy-start.7 = (f32[2,128,2,128,1]{1,3,0,2,4:T(8,128)S(1)}, f32[2,128,2,128,1]{1,3,0,2,4:T(8,128)}, u32[]{:S(2)}) copy-start(f32[2,128,2,128,1]{1,3,0,2,4:T(8,128)} %constant.99) | copy-start | bytes 786436
  192.4 1.6 copy-start.10
  192.4 14.1 %collective-permute-start.2 = (f32[2,4,128,128]{2,3,0,1:T(8,128)S(1)}, f32[2,4,128,128]{2,3,0,1:T(8,128)S(1)}, u32[]{:S(2)}, u32[]{:S(2)}) collective-permute-start(f32[2,4,128,128]{2,3,0,1:T(8,128)S(1)} %multiply_add_fusion), channel_id=1, source_target_pairs={{0,16},{8,24},{16,0},{24,8},{1,17},{9,25},{17,1},{25,9},{2,18},{10... | collective-permute-start | bytes 1572872 | tf_op jit(solution)/shard_map/ppermute | solution.py:46
  207.6 0.8 copy-start.8
  207.6 1.0 copy-start.9
  207.7 2.9 collective-permute-start.3
  208.6 3.7 %copy-start.15 = (f32[2,128,2,128,1]{3,1,0,2,4:T(8,128)S(1)}, f32[2,128,2,128,1]{3,1,0,2,4:T(8,128)}, u32[]{:S(2)}) copy-start(f32[2,128,2,128,1]{3,1,0,2,4:T(8,128)} %constant.100) | copy-start | bytes 786436
  218.1 52.1 %all-to-all-start.5 = ((f32[2,16,128,128]{3,0,1,2:T(2,128)}), f32[2,16,128,128]{3,0,1,2:T(2,128)}, u32[]{:S(2)}, u32[]{:S(2)}) async-start(f32[2,16,128,128]{3,0,1,2:T(2,128)} %copy.112), calls=%async_computation.5 | async-start | bytes 4194304 | tf_op jit(solution)/shard_map/all_to_all | solution.py:135
  270.2 52.2 %all-to-all-start.4 = ((f32[2,16,128,128]{3,0,1,2:T(2,128)}), f32[2,16,128,128]{3,0,1,2:T(2,128)S(1)}, u32[]{:S(2)}, u32[]{:S(2)}) async-start(f32[2,16,128,128]{3,0,1,2:T(2,128)} %copy.108), calls=%async_computation.4 | async-start | bytes 4194304 | tf_op jit(solution)/shard_map/all_to_all | solution.py:135
  322.4 1.6 copy-start.3
  322.4 1.6 copy-start.11
  326.8 4.5 %copy-start.1 = (f32[16,128,128]{2,1,0:T(8,128)S(1)}, f32[16,128,128]{2,1,0:T(8,128)}, u32[]{:S(2)}) copy-start(f32[16,128,128]{2,1,0:T(8,128)} %param.23) | copy-start | bytes 3145732

commit v2 on v1

--- a/solution.py
+++ b/solution.py
@@ -1,9 +1,13 @@
+import functools
 import math
 
 import jax
 import jax.numpy as jnp
+import ml_dtypes
 import numpy as np
 from jax import lax
+from jax.experimental import pallas as pl
+from jax.experimental.pallas import tpu as pltpu
 from jax.sharding import PartitionSpec as P
 
 high = lax.Precision.HIGH
@@ -18,6 +22,235 @@
     sine = direction * np.sin(angles) / math.sqrt(length)
     pairs = (np.stack((cosine, sine), axis=1), np.stack((-sine, cosine), axis=1))
     return np.stack(pairs, axis=0).astype(np.float32)
+
+
+def halves(values):
+    upper = values.astype(jnp.bfloat16)
+    return upper, (values - upper.astype(jnp.float32)).astype(jnp.bfloat16)
+
+
+def table_halves(table):
+    values = table.reshape(2 * table.shape[1], -1)
+    upper = values.astype(ml_dtypes.bfloat16)
+    lower = (values - upper.astype(np.float32)).astype(ml_dtypes.bfloat16)
+    return np.stack((upper, lower))
+
+
+def dot(first, second):
+    return jnp.dot(first, second, preferred_element_type=jnp.float32)
+
+
+def times_table(values, table):
+    upper, lower = halves(values)
+    return dot(upper, table[0]) + (dot(upper, table[1]) + dot(lower, table[0]))
+
+
+def table_times(table, values):
+    upper, lower = halves(values)
+    return dot(table[0], upper) + (dot(table[1], upper) + dot(table[0], lower))
+
+
+def meet(group, devices):
+    me = lax.axis_index(group)
+    barrier = pltpu.get_barrier_semaphore()
+    for step in range(1, devices):
+        peer = lax.rem(me + step, devices)
+        pl.semaphore_signal(
+            barrier, inc=1, device_id={group: peer}, device_id_type=pl.DeviceIdType.MESH
+        )
+    pl.semaphore_wait(barrier, devices - 1)
+    return me
+
+
+def arrive_kernel(grids, resp, orbital, left_x, right_z, left_y, out, away, here, sent, got, own):
+    rows, length = orbital.shape[0], orbital.shape[1]
+    block = rows * rows
+    me = meet("grid", grids)
+    copies = []
+    for harmonic in range(2):
+
+        def transform_x(pair, carry):
+            column = []
+            for k in range(2):
+                picked = pl.ds(2 * pair + k, length, stride=rows)
+                column.append(
+                    jnp.concatenate([resp[harmonic, c, picked, :] for c in range(2)], axis=0)
+                )
+            wave = table_times(left_x, jnp.concatenate(column, axis=1))
+            for k in range(2):
+                picked = pl.ds(2 * pair + k, length, stride=rows)
+                for c in range(2):
+                    away[harmonic, c, picked, :] = wave[
+                        c * length : (c + 1) * length, k * length : (k + 1) * length
+                    ]
+            return carry
+
+        lax.fori_loop(0, rows // 2, transform_x, 0)
+        mine = pltpu.make_async_copy(
+            away.at[harmonic, :, pl.ds(pl.multiple_of(me * block, block), block), :],
+            here.at[harmonic, me],
+            own.at[harmonic],
+        )
+        mine.start()
+        steps = []
+        for step in range(1, grids):
+            peer = lax.rem(me + step, grids)
+            copy = pltpu.make_async_remote_copy(
+                src_ref=away.at[
+                    harmonic, :, pl.ds(pl.multiple_of(peer * block, block), block), :
+                ],
+                dst_ref=here.at[harmonic, me],
+                send_sem=sent.at[harmonic, step],
+                recv_sem=got.at[harmonic, step],
+                device_id={"grid": peer},
+                device_id_type=pl.DeviceIdType.MESH,
+            )
+            copy.start()
+            steps.append(copy)
+        copies.append((mine, steps))
+    for harmonic in range(2):
+        mine, steps = copies[harmonic]
+        mine.wait()
+        for copy in steps:
+            copy.wait_recv()
+
+        def transform_zy(pair, carry):
+            lines = []
+            for k in range(2):
+                at = pl.ds(pl.multiple_of((2 * pair + k) * rows, rows), rows)
+                lines.append(
+                    jnp.concatenate(
+                        [
+                            jnp.concatenate(
+                                [here[harmonic, s, c, at, :] for s in range(grids)], axis=0
+                            )
+                            for c in range(2)
+                        ],
+                        axis=1,
+                    )
+                )
+            wave = times_table(jnp.concatenate(lines, axis=0), right_z)
+            planes = []
+            for k in range(2):
+                line = wave[k * length : (k + 1) * length]
+                planes.append(
+                    jnp.concatenate([line[:, :length], line[:, length:]], axis=0)
+                )
+            cell = table_times(left_y.at[harmonic], jnp.concatenate(planes, axis=1))
+            for k in range(2):
+                plane = 2 * pair + k
+                for c in range(2):
+                    value = cell[c * length : (c + 1) * length, k * length : (k + 1) * length]
+                    if harmonic == 0:
+                        out[c, plane] = value
+                    else:
+                        out[c, plane] = (out[c, plane] + value) * orbital[plane]
+            return carry
+
+        lax.fori_loop(0, rows // 2, transform_zy, 0)
+    for mine, steps in copies:
+        for copy in steps:
+            copy.wait_send()
+
+
+def leave_kernel(grids, pot, orbital, left_y, right_z, left_x, out, away, here, sent, got, own):
+    rows, length = orbital.shape[0], orbital.shape[1]
+    block = rows * rows
+    me = meet("grid", grids)
+    copies = []
+    for harmonic in range(2):
+
+        def transform_yz(pair, carry):
+            planes = []
+            for k in range(2):
+                plane = 2 * pair + k
+                weight = orbital[plane]
+                planes.append(
+                    jnp.concatenate([pot[c, plane] * weight for c in range(2)], axis=0)
+                )
+            wave = table_times(left_y.at[harmonic], jnp.concatenate(planes, axis=1))
+            lines = []
+            for k in range(2):
+                part = wave[:, k * length : (k + 1) * length]
+                lines.append(jnp.concatenate([part[:length], part[length:]], axis=1))
+            wave = times_table(jnp.concatenate(lines, axis=0), right_z)
+            for k in range(2):
+                at = pl.ds(pl.multiple_of((2 * pair + k) * rows, rows), rows)
+                for s in range(grids):
+                    first = k * length + s * rows
+                    for c in range(2):
+                        away[harmonic, s, c, at, :] = wave[
+                            first : first + rows, c * length : (c + 1) * length
+                        ]
+            return carry
+
+        lax.fori_loop(0, rows // 2, transform_yz, 0)
+        at_me = pl.ds(pl.multiple_of(me * block, block), block)
+        mine = pltpu.make_async_copy(
+            away.at[harmonic, me], here.at[harmonic, :, at_me, :], own.at[harmonic]
+        )
+        mine.start()
+        steps = []
+        for step in range(1, grids):
+            peer = lax.rem(me + step, grids)
+            copy = pltpu.make_async_remote_copy(
+                src_ref=away.at[harmonic, peer],
+                dst_ref=here.at[harmonic, :, at_me, :],
+                send_sem=sent.at[harmonic, step],
+                recv_sem=got.at[harmonic, step],
+                device_id={"grid": peer},
+                device_id_type=pl.DeviceIdType.MESH,
+            )
+            copy.start()
+            steps.append(copy)
+        copies.append((mine, steps))
+    for harmonic in range(2):
+        mine, steps = copies[harmonic]
+        mine.wait()
+        for copy in steps:
+            copy.wait_recv()
+
+        def transform_x(pair, carry):
+            column = []
+            for k in range(2):
+                picked = pl.ds(2 * pair + k, length, stride=rows)
+                column.append(
+                    jnp.concatenate([here[harmonic, c, picked, :] for c in range(2)], axis=0)
+                )
+            wave = table_times(left_x, jnp.concatenate(column, axis=1))
+            for k in range(2):
+                picked = pl.ds(2 * pair + k, length, stride=rows)
+                for c in range(2):
+                    out[harmonic, c, picked, :] = wave[
+                        c * length : (c + 1) * length, k * length : (k + 1) * length
+                    ]
+            return carry
+
+        lax.fori_loop(0, rows // 2, transform_x, 0)
+    for mine, steps in copies:
+        for copy in steps:
+            copy.wait_send()
+
+
+def call(kernel, grids, rows, length, out_shape, by_source, collective_id, *operands):
+    flat = (2, 2, length * rows, length)
+    blocks = (2, grids, 2, rows * rows, length)
+    return pl.pallas_call(
+        functools.partial(kernel, grids),
+        out_shape=jax.ShapeDtypeStruct(out_shape, jnp.float32),
+        in_specs=[pl.BlockSpec(memory_space=pltpu.VMEM)] * len(operands),
+        out_specs=pl.BlockSpec(memory_space=pltpu.VMEM),
+        scratch_shapes=[
+            pltpu.VMEM(flat if by_source else blocks, jnp.float32),
+            pltpu.VMEM(blocks if by_source else flat, jnp.float32),
+            pltpu.SemaphoreType.DMA((2, grids)),
+            pltpu.SemaphoreType.DMA((2, grids)),
+            pltpu.SemaphoreType.DMA((2,)),
+        ],
+        compiler_params=pltpu.CompilerParams(
+            collective_id=collective_id, has_side_effects=True, vmem_limit_bytes=40 * 2**20
+        ),
+    )(*operands)
 
 
 def ein(form, operand, table):
@@ -70,16 +303,20 @@
     backward = dft_pair(grid_len, 1.0)
     orbital = ground[0]
 
-    flip = np.array([1.0, -1.0], np.float32)[None, None, :, None]
-    partial = None
-    for harmonic in range(2):
-        table = backward if harmonic == 0 else backward * flip
-        wave = ein("cxyz,cxdk->dkyz", response[0, harmonic], backward)
-        wave = lax.all_to_all(wave, "grid", split_axis=1, concat_axis=2, tiled=True)
-        wave = ein("dxkz,dzem->exkm", wave, backward)
-        cell = ein("cxyz,cydk->dxkz", wave, table)
-        partial = cell if partial is None else partial + cell
-    partial = partial * orbital
+    flip = np.array([1.0, -1.0], np.float32)
+    turn = (2, 3, 0, 1)
+    left_y = np.stack([
+        table_halves(backward.transpose(turn)),
+        table_halves((backward * flip[:, None]).transpose(turn)),
+    ])
+    partial = call(
+        arrive_kernel, grids, planes, grid_len, (2, planes, grid_len, grid_len), True, 0,
+        response.reshape(2, 2, grid_len * planes, grid_len),
+        orbital,
+        table_halves(backward.transpose(turn)),
+        table_halves(backward),
+        left_y,
+    )
 
     me_band = lax.axis_index("band")
     if planes % bands == 0 and bands & (bands - 1) == 0:
@@ -126,15 +363,15 @@
         pot = hartree(dens, "grid", lax.axis_index("grid"), grids, None)
         pot = pot + kernel_xc * dens
 
-    prod = pot * orbital
-    outs = []
-    for harmonic in range(2):
-        table = forward if harmonic == 0 else forward * flip.reshape(2, 1, 1, 1)
-        wave = ein("cxyz,cydk->dxkz", prod, table)
-        wave = ein("dxkz,dzem->exkm", wave, forward)
-        wave = lax.all_to_all(wave, "grid", split_axis=2, concat_axis=1, tiled=True)
-        outs.append(ein("cxyz,cxdk->dkyz", wave, forward))
-    return jnp.stack(outs, axis=0)[None]
+    left_y = np.stack([
+        table_halves(forward.transpose(turn)),
+        table_halves((forward * flip[:, None, None, None]).transpose(turn)),
+    ])
+    out = call(
+        leave_kernel, grids, planes, grid_len, (2, 2, grid_len * planes, grid_len), False, 1,
+        pot, orbital, left_y, table_halves(forward), table_halves(forward.transpose(turn)),
+    )
+    return out.reshape(1, 2, 2, grid_len, planes, grid_len)
 
 
 def solution(mesh):

time: 337 us -> 302 us (0.90); the launches traced: 331 us -> 301 us
  Pallas kernels: 0 us -> 207 us
  waiting for transfers between devices: 216 us -> 57.4 us
  starting transfers between devices: 43.7 us -> 14.5 us
  local copies, waits for them, and re-layouts: 39.6 us -> 14.5 us
  matrix products: 25.6 us -> 4.83 us
    pallas_call x0 -> x2, Pallas kernels: none -> 207 us  [call(): pl.pallas_call(functools.partial(kernel, grids), out_shape=jax.ShapeDtype...]
    all_to_all x4 -> x0, waiting for transfers between devices: 162 us -> none  [the longest x2 81.7 us: on_device(): wave = lax.all_to_all(wave, 'grid', split_axis=2, concat_axis=1, tiled=True)]
    all_to_all x4 -> x0, starting transfers between devices: 27.5 us -> none  [the longest x2 13.8 us: on_device(): wave = lax.all_to_all(wave, 'grid', split_axis=1, concat_axis=2, tiled=True)]
    dot_general x18 -> x6, matrix products: 25.6 us -> 4.83 us  [ein(): return jnp.einsum(form, operand, table, precision=high)]
    all_to_all x4 -> x0, local copies, waits for them, and re-layouts: 8.63 us -> none  [the longest x2 5.21 us: on_device(): wave = lax.all_to_all(wave, 'grid', split_axis=1, concat_axis=2, tiled=True)]
    unnamed x34 -> x33, local copies, waits for them, and re-layouts: 3.73 us -> 10.8 us
    transpose x3 -> x1, local copies, waits for them, and re-layouts: 7.08 us -> 1.21 us  [ein(): return jnp.einsum(form, operand, table, precision=high)]
    dot_general x3 -> x1, local copies, waits for them, and re-layouts: 6.21 us -> 1.14 us  [ein(): return jnp.einsum(form, operand, table, precision=high)]
  transfers between devices with their start and end apart: 10 -> 6, of which waited for: 10 -> 6; matrix products, arithmetic and copies ran while one was open for 6% -> 0% of each run, Pallas kernels for 0% -> 0%
where the time goes in v2:
time: 302 us; the launch traced here: 301 us
  Pallas kernels  207 us (69%)
  waiting for transfers between devices  57.4 us (19%)
  local copies, waits for them, and re-layouts  14.5 us (5%)
  starting transfers between devices  14.5 us (5%)
  matrix products  4.83 us (2%)
    pallas_call x2, Pallas kernels, call(): pl.pallas_call(functools.partial(kernel, grids), out_shape=jax.ShapeDtype...  207 us
    ppermute x4, waiting for transfers between devices, swap(): return lax.ppermute(values, 'band', [(i, i ^ bit) for i in range(size)])  30.8 us
    all_to_all x1, waiting for transfers between devices, hartree(): wave = lax.all_to_all(wave, axes, split_axis=1, concat_axis=2, tiled=True)  13.4 us
    all_to_all x1, waiting for transfers between devices, hartree(): wave = lax.all_to_all(wave, axes, split_axis=2, concat_axis=1, tiled=True)  13.2 us
    unnamed x33, local copies, waits for them, and re-layouts  10.8 us
  transfers between devices with their start and end apart: 6, of which 6 were waited for; matrix products, arithmetic and copies ran while one was open for 0% of the time, Pallas kernels for 0%

profile of v2, /device:TPU:10, one launch (start us, length us, event | category | flops | bytes accessed | tf_op | source)
XLA Modules:
  0.0 301.4 jit_solution(7132796407681858426)
XLA Ops:
  0.0 2.3 copy-done.1
  2.3 1.2 copy-done.2
  3.5 0.9 copy-done.4
  4.5 0.9 copy-done.6
  5.4 1.0 copy-done.9
  6.4 103.1 %shard_map.145 = f32[2,16,128,128]{3,2,1,0:T(8,128)S(1)} custom-call(f32[2,2,2048,128]{3,2,1,0:T(8,128)S(1)} %bitcast.74, f32[16,128,128]{2,1,0:T(8,128)S(1)} %bitcast.75, bf16[2,256,256]{2,1,0:T(8,128)(2,1)S(1)} %copy-done.6, bf16[2,256,256]{2,1,0:T(8,128)(2,1)S(1)} %copy-done.4, bf16[2,2,256,256]{3,2,1,0:T(8,128)(2,1)S(1)} %copy-done.9), custom_call_target="tpu_custom_call" | custom-call | tf_op jit(solution)/shard_map/pallas_call | solution.py:238
  109.5 1.0 constant_dynamic-slice_fusion.2
  110.6 3.0 collective-permute-done
  113.6 1.3 dynamic-slice_add_fusion
  114.9 1.0 copy-done.10
  115.9 1.6 collective-permute-start.1
  117.5 12.4 %collective-permute-done.1 = f32[2,4,128,128]{3,2,1,0:T(8,128)S(1)} collective-permute-done((f32[2,4,128,128]{3,2,1,0:T(8,128)S(1)}, f32[2,4,128,128]{3,2,1,0:T(8,128)S(1)}, u32[]{:S(2)}, u32[]{:S(2)}) %collective-permute-start.1) | collective-permute-done | bytes 524320 | tf_op jit(solution)/shard_map/ppermute | solution.py:279
  130.0 1.7 convolution_bitcast_fusion.5
  131.6 0.6 convolution_bitcast_fusion.4
  132.3 1.2 copy.22
  133.5 5.7 %all-to-all-start = ((f32[2,4,128,128]{3,0,1,2:T(2,128)}), f32[2,4,128,128]{3,0,1,2:T(2,128)S(1)}, u32[]{:S(2)}, u32[]{:S(2)}) async-start(f32[2,4,128,128]{3,0,1,2:T(2,128)} %copy.22), calls=%async_computation | async-start | bytes 1048576 | tf_op jit(solution)/shard_map/all_to_all | solution.py:287
  139.5 13.2 %all-to-all-done = f32[2,4,128,128]{3,0,1,2:T(2,128)S(1)} async-done(((f32[2,4,128,128]{3,0,1,2:T(2,128)}), f32[2,4,128,128]{3,0,1,2:T(2,128)S(1)}, u32[]{:S(2)}, u32[]{:S(2)}) %all-to-all-start) | async-done | bytes 524320 | tf_op jit(solution)/shard_map/all_to_all | solution.py:287
  152.8 0.4 fusion.1
  153.2 0.4 convolution_bitcast_fusion.2
  153.6 1.1 copy.25
  154.7 5.6 %all-to-all-start.1 = ((f32[2,128,4,128]{3,2,0,1:T(4,128)}), f32[2,128,4,128]{3,2,0,1:T(4,128)S(1)}, u32[]{:S(2)}, u32[]{:S(2)}) async-start(f32[2,128,4,128]{3,2,0,1:T(4,128)} %copy.25), calls=%async_computation.1 | async-start | bytes 1048576 | tf_op jit(solution)/shard_map/all_to_all | solution.py:294
  160.4 13.4 %all-to-all-done.1 = f32[2,128,4,128]{3,2,0,1:T(4,128)S(1)} async-done(((f32[2,128,4,128]{3,2,0,1:T(4,128)}), f32[2,128,4,128]{3,2,0,1:T(4,128)S(1)}, u32[]{:S(2)}, u32[]{:S(2)}) %all-to-all-start.1) | async-done | bytes 524320 | tf_op jit(solution)/shard_map/all_to_all | solution.py:294
  173.9 1.3 convolution_bitcast_fusion.1
  175.3 0.5 multiply_add_fusion
  175.7 1.6 collective-permute-start.2
  177.3 12.5 %collective-permute-done.2 = f32[2,4,128,128]{3,2,1,0:T(8,128)S(1)} collective-permute-done((f32[2,4,128,128]{3,2,1,0:T(8,128)S(1)}, f32[2,4,128,128]{3,2,1,0:T(8,128)S(1)}, u32[]{:S(2)}, u32[]{:S(2)}) %collective-permute-start.2) | collective-permute-done | bytes 524320 | tf_op jit(solution)/shard_map/ppermute | solution.py:279
  189.9 1.0 pad_maximum_fusion.1
  191.0 2.9 collective-permute-done.3
  194.2 1.0 copy-done.3
  195.3 0.2 copy-done.8
  195.5 103.9 %shard_map.146 = f32[2,2,2048,128]{3,2,1,0:T(8,128)S(1)} custom-call(f32[2,16,128,128]{3,2,1,0:T(8,128)S(1)} %pad_maximum_fusion.pot, f32[16,128,128]{2,1,0:T(8,128)S(1)} %bitcast.76, bf16[2,2,256,256]{3,2,1,0:T(8,128)(2,1)S(1)} %copy-done.8, bf16[2,256,256]{2,1,0:T(8,128)(2,1)S(1)} %copy-done.7, bf16[2,256,256]{2,1,0:T(8,128)(2,1)S(1)} %copy-done.5), custom_call_target="tpu_custom_call" | custom-call | tf_op jit(solution)/shard_map/pallas_call | solution.py:238
  299.4 2.0 copy.60
  (37 shorter events, 1.1 us)
Async XLA Ops:
  0.0 160.3 %copy-start = (f32[16,128,128]{2,1,0:T(8,128)S(1)}, f32[16,128,128]{2,1,0:T(8,128)}, u32[]{:S(2)}) copy-start(f32[16,128,128]{2,1,0:T(8,128)} %param.17) | copy-start | bytes 3145732
  0.0 2.3 copy-start.1
  2.3 1.2 copy-start.2
  3.5 0.9 copy-start.4
  4.5 0.9 copy-start.6
  5.4 1.0 copy-start.9
  110.6 3.0 collective-permute-start
  110.6 19.4 %copy-start.12 = (f32[2,128,2,128,1]{3,1,0,2,4:T(8,128)S(1)}, f32[2,128,2,128,1]{3,1,0,2,4:T(8,128)}, u32[]{:S(2)}) copy-start(f32[2,128,2,128,1]{3,1,0,2,4:T(8,128)} %constant.106) | copy-start | bytes 786436
  114.9 1.0 copy-start.10
  115.9 14.0 %collective-permute-start.1 = (f32[2,4,128,128]{3,2,1,0:T(8,128)S(1)}, f32[2,4,128,128]{3,2,1,0:T(8,128)S(1)}, u32[]{:S(2)}, u32[]{:S(2)}) collective-permute-start(f32[2,4,128,128]{3,2,1,0:T(8,128)S(1)} %constant_dynamic-slice_fusion.1), channel_id=1, source_target_pairs={{0,16},{8,24},{16,0},{24,8},{1,17},{9,25},{17,1},{25,9},{2,18},{10... | collective-permute-start | bytes 1572872 | tf_op jit(solution)/shard_map/ppermute | solution.py:279
  131.6 21.1 %copy-start.14 = (f32[2,128,2,128,1]{1,3,0,2,4:T(8,128)S(1)}, f32[2,128,2,128,1]{1,3,0,2,4:T(8,128)}, u32[]{:S(2)}) copy-start(f32[2,128,2,128,1]{1,3,0,2,4:T(8,128)} %constant.105) | copy-start | bytes 786436
  133.5 19.7 %copy-start.13 = (f32[2,128,2,128,1]{1,3,0,4,2:T(8,128)S(1)}, f32[2,128,2,128,1]{1,3,0,4,2:T(8,128)}, u32[]{:S(2)}) copy-start(f32[2,128,2,128,1]{1,3,0,4,2:T(8,128)} %constant.104) | copy-start | bytes 786436
  133.5 19.2 %all-to-all-start = ((f32[2,4,128,128]{3,0,1,2:T(2,128)}), f32[2,4,128,128]{3,0,1,2:T(2,128)S(1)}, u32[]{:S(2)}, u32[]{:S(2)}) async-start(f32[2,4,128,128]{3,0,1,2:T(2,128)} %copy.22), calls=%async_computation | async-start | bytes 1048576 | tf_op jit(solution)/shard_map/all_to_all | solution.py:287
  154.7 20.5 %copy-start.11 = (f32[2,8,128,128]{3,2,1,0:T(8,128)S(1)}, f32[2,8,128,128]{3,2,1,0:T(8,128)}, u32[]{:S(2)}) copy-start(f32[2,8,128,128]{3,2,1,0:T(8,128)} %copy-done.10) | copy-start | bytes 3145732
  154.7 19.1 %all-to-all-start.1 = ((f32[2,128,4,128]{3,2,0,1:T(4,128)}), f32[2,128,4,128]{3,2,0,1:T(4,128)S(1)}, u32[]{:S(2)}, u32[]{:S(2)}) async-start(f32[2,128,4,128]{3,2,0,1:T(4,128)} %copy.25), calls=%async_computation.1 | async-start | bytes 1048576 | tf_op jit(solution)/shard_map/all_to_all | solution.py:294
  173.8 1.5 copy-start.15
  175.7 14.1 %collective-permute-start.2 = (f32[2,4,128,128]{3,2,1,0:T(8,128)S(1)}, f32[2,4,128,128]{3,2,1,0:T(8,128)S(1)}, u32[]{:S(2)}, u32[]{:S(2)}) collective-permute-start(f32[2,4,128,128]{3,2,1,0:T(8,128)S(1)} %multiply_add_fusion), channel_id=1, source_target_pairs={{0,16},{8,24},{16,0},{24,8},{1,17},{9,25},{17,1},{25,9},{2,18},{10... | collective-permute-start | bytes 1572872 | tf_op jit(solution)/shard_map/ppermute | solution.py:279
  191.0 2.9 collective-permute-start.3
  194.0 1.2 copy-start.3
  194.0 1.3 copy-start.5
  194.0 1.3 copy-start.7
  194.0 1.5 copy-start.8

commit v3 on v2

--- a/solution.py
+++ b/solution.py
@@ -232,6 +232,208 @@
             copy.wait_send()
 
 
+def middle_kernel(
+    grids, part, kernel, weights, front_y, right_front, front_x, back_x, back_y, right_back, out,
+    got_half, half, got_own, dens, away, here, back_away, back_here, pair_sent, pair_got, sent, got,
+):
+    devices = 4 * grids
+    planes, length = part.shape[1], part.shape[2]
+    own = planes // 4
+    rows = length // devices
+    block = 2 * own * rows
+    band, grid = lax.axis_index("band"), lax.axis_index("grid")
+    me = band * grids + grid
+
+    def at(device):
+        return {"band": device // grids, "grid": lax.rem(device, grids)}
+
+    barrier = pltpu.get_barrier_semaphore()
+
+    def greet(step, carry):
+        pl.semaphore_signal(
+            barrier, inc=1, device_id=at(lax.rem(me + step, devices)),
+            device_id_type=pl.DeviceIdType.MESH,
+        )
+        return carry
+
+    lax.fori_loop(1, devices, greet, 0)
+    pl.semaphore_wait(barrier, devices - 1)
+
+    low_bit, high_bit = lax.rem(band, 2), band // 2
+    near = {"band": 2 * high_bit + (1 - low_bit), "grid": grid}
+    far = {"band": 2 * (1 - high_bit) + low_bit, "grid": grid}
+
+    def pair_copy(source, target, place, index):
+        return pltpu.make_async_remote_copy(
+            src_ref=source, dst_ref=target, send_sem=pair_sent.at[index],
+            recv_sem=pair_got.at[index], device_id=place, device_id_type=pl.DeviceIdType.MESH,
+        )
+
+    first = pair_copy(part.at[:, pl.ds((1 - low_bit) * 2 * own, 2 * own)], got_half, near, 0)
+    first.start()
+    first.wait()
+
+    def add_half(plane, carry):
+        for c in range(2):
+            half[c, plane] = part[c, low_bit * 2 * own + plane] + got_half[c, plane]
+        return carry
+
+    lax.fori_loop(0, 2 * own, add_half, 0)
+    second = pair_copy(half.at[:, pl.ds((1 - high_bit) * own, own)], got_own, far, 1)
+    second.start()
+    second.wait()
+
+    def add_own(plane, carry):
+        for c in range(2):
+            dens[c, plane] = half[c, high_bit * own + plane] + got_own[c, plane]
+        return carry
+
+    lax.fori_loop(0, own, add_own, 0)
+
+    def exchange(source, target, index):
+        mine = pl.ds(pl.multiple_of(me * block, block), block)
+
+        def copy_of(step):
+            peer = lax.rem(me + step, devices)
+            return pltpu.make_async_remote_copy(
+                src_ref=source.at[pl.ds(pl.multiple_of(peer * block, block), block)],
+                dst_ref=target.at[mine],
+                send_sem=sent.at[index, step],
+                recv_sem=got.at[index, step],
+                device_id=at(peer),
+                device_id_type=pl.DeviceIdType.MESH,
+            )
+
+        def start(step, carry):
+            copy_of(step).start()
+            return carry
+
+        def finish(step, carry):
+            copy_of(step).wait()
+            return carry
+
+        lax.fori_loop(1, devices, start, 0)
+        target[mine, :] = source[mine, :]
+        lax.fori_loop(1, devices, finish, 0)
+
+    def lane(values, index):
+        return values[:, index * length : (index + 1) * length]
+
+    def beside(values):
+        lines = [
+            jnp.concatenate([lane(values, p)[:length], lane(values, p)[length:]], axis=1)
+            for p in range(own)
+        ]
+        return jnp.concatenate(lines, axis=0)
+
+    def spread(c, plane, row):
+        return pl.ds((c * own + plane) * rows + row, devices, stride=block)
+
+    field = jnp.concatenate(
+        [jnp.concatenate([dens[c, p] for c in range(2)], axis=0) for p in range(own)], axis=1
+    )
+    wave = times_table(beside(table_times(front_y, field)), right_front)
+    for p in range(own):
+        for row in range(rows):
+            top = p * length + row * devices
+            for c in range(2):
+                away[spread(c, p, row), :] = lane(wave[top : top + devices], c)
+    exchange(away, here, 0)
+    field = jnp.concatenate(
+        [
+            jnp.concatenate(
+                [here[spread(c, p, row), :] for c in range(2) for p in range(own)], axis=0
+            )
+            for row in range(rows)
+        ],
+        axis=1,
+    )
+    wave = table_times(front_x, field)
+    weight = weights[...]
+    wave = jnp.concatenate([wave[:length] * weight, wave[length:] * weight], axis=0)
+    field = table_times(back_x, wave)
+    for row in range(rows):
+        for c in range(2):
+            for p in range(own):
+                top = (c * own + p) * devices
+                back_away[spread(c, p, row), :] = lane(field[top : top + devices], row)
+    exchange(back_away, back_here, 1)
+    wave = jnp.concatenate(
+        [
+            jnp.concatenate(
+                [back_here[spread(c, p, row), :] for c in range(2) for row in range(rows)], axis=0
+            )
+            for p in range(own)
+        ],
+        axis=1,
+    )
+    cell = times_table(beside(table_times(back_y, wave)), right_back)
+    low = (2 * low_bit + high_bit) * own
+    for p in range(own):
+        for c in range(2):
+            value = lane(cell[p * length : (p + 1) * length], c)
+            out[c, low + p] = value + kernel[low + p] * dens[c, p]
+
+    third = pair_copy(out.at[:, pl.ds(low, own)], out.at[:, pl.ds(low, own)], far, 2)
+    third.start()
+    third.wait()
+    whole = pl.ds(low_bit * 2 * own, 2 * own)
+    fourth = pair_copy(out.at[:, whole], out.at[:, whole], near, 3)
+    fourth.start()
+    fourth.wait()
+
+
+def middle(grids, partial, kernel_xc):
+    planes, length = partial.shape[1], partial.shape[2]
+    devices = 4 * grids
+    own, rows = planes // 4, length // devices
+    turn = (2, 3, 0, 1)
+    kept = np.arange(rows)[:, None] + rows * np.arange(devices)[None, :]
+    kept = kept.reshape(-1)
+    place = np.array([0, 2, 1, 3])
+    numbers = (
+        np.arange(own)[:, None, None]
+        + own * place[None, :, None]
+        + planes * np.arange(grids)[None, None, :]
+    ).reshape(-1)
+    mine = (lax.axis_index("band") * grids + lax.axis_index("grid")) * rows
+    freqs = signed_freq(jnp.arange(length, dtype=jnp.int32), length)
+    own_freqs = signed_freq(mine + jnp.arange(rows, dtype=jnp.int32), length)
+    weights = coulomb(freqs, own_freqs, freqs, length).reshape(length, rows * length)
+    operands = (
+        partial,
+        kernel_xc,
+        weights,
+        table_halves(dft_pair(length, -1.0, columns=kept).transpose(turn)),
+        table_halves(dft_pair(length, -1.0)),
+        table_halves(dft_pair(length, -1.0, rows=numbers).transpose(turn)),
+        table_halves(dft_pair(length, 1.0, columns=numbers).transpose(turn)),
+        table_halves(dft_pair(length, 1.0, rows=kept).transpose(turn)),
+        table_halves(dft_pair(length, 1.0)),
+    )
+    parts = pltpu.VMEM((2 * own * length, length), jnp.float32)
+    return pl.pallas_call(
+        functools.partial(middle_kernel, grids),
+        out_shape=jax.ShapeDtypeStruct(partial.shape, jnp.float32),
+        in_specs=[pl.BlockSpec(memory_space=pltpu.VMEM)] * len(operands),
+        out_specs=pl.BlockSpec(memory_space=pltpu.VMEM),
+        scratch_shapes=[
+            pltpu.VMEM((2, 2 * own, length, length), jnp.float32),
+            pltpu.VMEM((2, 2 * own, length, length), jnp.float32),
+            pltpu.VMEM((2, own, length, length), jnp.float32),
+            pltpu.VMEM((2, own, length, length), jnp.float32),
+            parts, parts, parts, parts,
+            pltpu.SemaphoreType.DMA((4,)),
+            pltpu.SemaphoreType.DMA((4,)),
+            pltpu.SemaphoreType.DMA((2, devices)),
+            pltpu.SemaphoreType.DMA((2, devices)),
+        ],
+        compiler_params=pltpu.CompilerParams(
+            collective_id=2, has_side_effects=True, vmem_limit_bytes=40 * 2**20
+        ),
+    )(*operands)
+
+
 def call(kernel, grids, rows, length, out_shape, by_source, collective_id, *operands):
     flat = (2, 2, length * rows, length)
     blocks = (2, grids, 2, rows * rows, length)
@@ -275,10 +477,6 @@
     )
 
 
-def swap(values, bit, size):
-    return lax.ppermute(values, "band", [(i, i ^ bit) for i in range(size)])
-
-
 def hartree(density, axes, device, devices, numbers):
     length = density.shape[-1]
     forward, backward = dft_pair(length, -1.0), dft_pair(length, 1.0)
@@ -318,46 +516,8 @@
         left_y,
     )
 
-    me_band = lax.axis_index("band")
-    if planes % bands == 0 and bands & (bands - 1) == 0:
-        dens = partial
-        kernel = kernel_xc
-        bit = bands // 2
-        bits = []
-        while bit >= 1:
-            bits.append(bit)
-            bit //= 2
-        steps = list(reversed(bits))
-        low = jnp.int32(0)
-        for bit in steps:
-            half = dens.shape[1] // 2
-            mine = (me_band // bit) % 2
-            keep = lax.dynamic_slice_in_dim(dens, mine * half, half, 1)
-            give = lax.dynamic_slice_in_dim(dens, (1 - mine) * half, half, 1)
-            dens = keep + swap(give, bit, bands)
-            low = low + mine * half
-        own = dens.shape[1]
-        kernel = lax.dynamic_slice_in_dim(kernel_xc, low, own, 0)
-        place = [0] * bands
-        for b in range(bands):
-            size = planes
-            for bit in steps:
-                size //= 2
-                place[b] += ((b // bit) % 2) * (size // own)
-        numbers = (
-            np.arange(grids)[None, :, None] * planes
-            + np.array(place)[:, None, None] * own
-            + np.arange(own)[None, None, :]
-        ).reshape(-1)
-        device = me_band * grids + lax.axis_index("grid")
-        pot = hartree(dens, ("band", "grid"), device, bands * grids, numbers)
-        pot = pot + kernel * dens
-        for bit in reversed(steps):
-            mine = (me_band // bit) % 2
-            other = swap(pot, bit, bands)
-            first = jnp.where(mine == 0, pot, other)
-            second = jnp.where(mine == 0, other, pot)
-            pot = jnp.concatenate((first, second), axis=1)
+    if bands == 4 and planes % 4 == 0 and grid_len % (4 * grids) == 0:
+        pot = middle(grids, partial, kernel_xc)
     else:
         dens = lax.psum(partial, "band")
         pot = hartree(dens, "grid", lax.axis_index("grid"), grids, None)

time: 302 us -> 281 us (0.930)
  Pallas kernels: 207 us -> 272 us
  waiting for transfers between devices: 57.4 us -> 0 us
  starting transfers between devices: 14.5 us -> 0 us
  local copies, waits for them, and re-layouts: 14.5 us -> 8.61 us
  matrix products: 4.83 us -> 0 us
    pallas_call x0 -> x1, Pallas kernels: none -> 66.2 us  [middle(): pl.pallas_call(functools.partial(middle_kernel, grids), out_shape=jax.Sha...]
    ppermute x4 -> x0, waiting for transfers between devices: 30.8 us -> none  [swap(): return lax.ppermute(values, 'band', [(i, i ^ bit) for i in range(size)])]
    all_to_all x2 -> x0, waiting for transfers between devices: 26.6 us -> none  [the longest x1 13.4 us: hartree(): wave = lax.all_to_all(wave, axes, split_axis=1, concat_axis=2, tiled=True)]
    all_to_all x2 -> x0, starting transfers between devices: 11.3 us -> none  [the longest x1 5.71 us: hartree(): wave = lax.all_to_all(wave, axes, split_axis=2, concat_axis=1, tiled=True)]
    dot_general x6 -> x0, matrix products: 4.83 us -> none  [ein(): return jnp.einsum(form, operand, table, precision=high)]
    ppermute x4 -> x0, starting transfers between devices: 3.17 us -> none  [swap(): return lax.ppermute(values, 'band', [(i, i ^ bit) for i in range(size)])]
    unnamed x33 -> x29, local copies, waits for them, and re-layouts: 10.8 us -> 8.41 us
  transfers between devices with their start and end apart: 6 -> 0, of which waited for: 6 -> 0; matrix products, arithmetic and copies ran while one was open for 0% -> 0% of each run, Pallas kernels for 0% -> 0%
where the time goes in v3:
time: 281 us
  Pallas kernels  272 us (97%)
  local copies, waits for them, and re-layouts  8.61 us (3%)
    pallas_call x2, Pallas kernels, call(): pl.pallas_call(functools.partial(kernel, grids), out_shape=jax.ShapeDtype...  206 us
    pallas_call x1, Pallas kernels, middle(): pl.pallas_call(functools.partial(middle_kernel, grids), out_shape=jax.Sha...  66.2 us
    unnamed x29, local copies, waits for them, and re-layouts  8.41 us

profile of v3, /device:TPU:10, one launch (start us, length us, event | category | flops | bytes accessed | tf_op | source)
XLA Modules:
  0.0 280.8 jit_solution(12388758488242749911)
XLA Ops:
  0.0 0.1 broadcast_add_fusion
  0.1 0.2 add.71
  0.3 0.1 divide_select_fusion.weights
  0.4 0.0 copy-start
  0.4 2.2 copy-done
  2.6 0.0 copy-start.1
  2.6 1.2 copy-done.1
  3.8 0.0 copy-start.3
  3.8 0.9 copy-done.3
  4.8 0.0 copy-start.5
  4.8 0.9 copy-done.5
  5.7 0.0 copy-start.9
  5.7 1.0 copy-done.9
  6.7 0.0 copy-start.7
  6.8 0.0 copy-start.13
  6.8 103.2 %shard_map.145.part = f32[2,16,128,128]{3,2,1,0:T(8,128)S(1)} custom-call(f32[2,2,2048,128]{3,2,1,0:T(8,128)S(1)} %bitcast.11, f32[16,128,128]{2,1,0:T(8,128)S(1)} %bitcast.12, bf16[2,256,256]{2,1,0:T(8,128)(2,1)S(1)} %copy-done.5, bf16[2,256,256]{2,1,0:T(8,128)(2,1)S(1)} %copy-done.3, bf16[2,2,256,256]{3,2,1,0:T(8,128)(2,1)S(1)} %copy-done.9), custom_call_target="tpu_custom_call" | custom-call | tf_op jit(solution)/shard_map/pallas_call | solution.py:440
  110.0 0.0 copy-done.7
  110.0 0.0 copy-done.10
  110.0 0.0 copy-done.11
  110.0 0.0 copy-done.12
  110.0 0.0 copy-done.13
  110.0 0.0 copy-start.2
  110.0 0.0 copy-start.4
  110.0 0.0 copy-start.6
  110.0 0.0 copy-start.8
  110.1 66.2 %shard_map.146.pot = f32[2,16,128,128]{3,2,1,0:T(8,128)S(1)} custom-call(f32[2,16,128,128]{3,2,1,0:T(8,128)S(1)} %shard_map.145.part, f32[16,128,128]{2,1,0:T(8,128)S(1)} %copy-done.7, f32[128,512]{1,0:T(8,128)S(1)} %divide_select_fusion.weights, bf16[2,256,256]{2,1,0:T(8,128)(2,1)S(1)} %copy-done.13, bf16[2,256,256]{2,1,0:T(8,128)(2,1)S(1)} %copy-done.5, ...), custom_call_target="tpu_custom_call" | custom-call | tf_op jit(solution)/shard_map/pallas_call | solution.py:415
  176.3 0.0 copy-done.2
  176.3 0.0 copy-done.4
  176.3 0.0 copy-done.6
  176.3 0.0 copy-done.8
  176.3 102.4 %shard_map.147 = f32[2,2,2048,128]{3,2,1,0:T(8,128)S(1)} custom-call(f32[2,16,128,128]{3,2,1,0:T(8,128)S(1)} %shard_map.146.pot, f32[16,128,128]{2,1,0:T(8,128)S(1)} %bitcast.13, bf16[2,2,256,256]{3,2,1,0:T(8,128)(2,1)S(1)} %copy-done.8, bf16[2,256,256]{2,1,0:T(8,128)(2,1)S(1)} %copy-done.6, bf16[2,256,256]{2,1,0:T(8,128)(2,1)S(1)} %copy-done.4), custom_call_target="tpu_custom_call" | custom-call | tf_op jit(solution)/shard_map/pallas_call | solution.py:440
  278.7 2.0 copy.21
  (6 shorter events, 0.0 us)
Async XLA Ops:
  0.4 2.2 copy-start
  2.6 1.2 copy-start.1
  3.8 0.9 copy-start.3
  4.8 0.9 copy-start.5
  5.7 1.0 copy-start.9
  6.7 103.2 %copy-start.7 = (f32[16,128,128]{2,1,0:T(8,128)S(1)}, f32[16,128,128]{2,1,0:T(8,128)}, u32[]{:S(2)}) copy-start(f32[16,128,128]{2,1,0:T(8,128)} %kernel.1) | copy-start | bytes 3145732
  6.7 103.2 %copy-start.10 = (bf16[2,256,256]{2,1,0:T(8,128)(2,1)S(1)}, bf16[2,256,256]{2,1,0:T(8,128)(2,1)}, u32[]{:S(2)}) copy-start(bf16[2,256,256]{2,1,0:T(8,128)(2,1)} %constant.52.clone.back_y) | copy-start | bytes 786436
  6.7 103.2 %copy-start.11 = (bf16[2,256,256]{2,1,0:T(8,128)(2,1)S(1)}, bf16[2,256,256]{2,1,0:T(8,128)(2,1)}, u32[]{:S(2)}) copy-start(bf16[2,256,256]{2,1,0:T(8,128)(2,1)} %constant.51.clone.back_x) | copy-start | bytes 786436
  6.8 103.2 %copy-start.12 = (bf16[2,256,256]{2,1,0:T(8,128)(2,1)S(1)}, bf16[2,256,256]{2,1,0:T(8,128)(2,1)}, u32[]{:S(2)}) copy-start(bf16[2,256,256]{2,1,0:T(8,128)(2,1)} %constant.50.clone.front_x) | copy-start | bytes 786436
  6.8 103.2 %copy-start.13 = (bf16[2,256,256]{2,1,0:T(8,128)(2,1)S(1)}, bf16[2,256,256]{2,1,0:T(8,128)(2,1)}, u32[]{:S(2)}) copy-start(bf16[2,256,256]{2,1,0:T(8,128)(2,1)} %constant.49.clone.front_y) | copy-start | bytes 786436
  110.0 66.3 %copy-start.2 = (f32[1,16,128,128]{3,2,1,0:T(8,128)S(1)}, f32[1,16,128,128]{3,2,1,0:T(8,128)}, u32[]{:S(2)}) copy-start(f32[1,16,128,128]{3,2,1,0:T(8,128)} %param.15) | copy-start | bytes 3145732
  110.0 66.3 %copy-start.4 = (bf16[2,256,256]{2,1,0:T(8,128)(2,1)S(1)}, bf16[2,256,256]{2,1,0:T(8,128)(2,1)}, u32[]{:S(2)}) copy-start(bf16[2,256,256]{2,1,0:T(8,128)(2,1)} %constant.47.clone.right_z.right_back.left_x) | copy-start | bytes 786436
  110.0 66.3 %copy-start.6 = (bf16[2,256,256]{2,1,0:T(8,128)(2,1)S(1)}, bf16[2,256,256]{2,1,0:T(8,128)(2,1)}, u32[]{:S(2)}) copy-start(bf16[2,256,256]{2,1,0:T(8,128)(2,1)} %constant.46.clone.left_x.right_front.right_z) | copy-start | bytes 786436
  110.0 66.3 %copy-start.8 = (bf16[2,2,256,256]{3,2,1,0:T(8,128)(2,1)S(1)}, bf16[2,2,256,256]{3,2,1,0:T(8,128)(2,1)}, u32[]{:S(2)}) copy-start(bf16[2,2,256,256]{3,2,1,0:T(8,128)(2,1)} %constant.53.clone.left_y) | copy-start | bytes 1572868

commit v4 on v3

v4 whole, which is shorter than its diff:
```python
import functools
import math

import jax
import jax.numpy as jnp
import ml_dtypes
import numpy as np
from jax import lax
from jax.experimental import pallas as pl
from jax.experimental.pallas import tpu as pltpu
from jax.sharding import PartitionSpec as P

high = lax.Precision.HIGH
spacing = 0.4527
width = 4


def dft_pair(length, direction, rows=None, columns=None):
    rows = np.arange(length) if rows is None else rows
    columns = np.arange(length) if columns is None else columns
    angles = (rows[:, None] * columns[None, :] % length) * (2.0 * math.pi / length)
    cosine = np.cos(angles) / math.sqrt(length)
    sine = direction * np.sin(angles) / math.sqrt(length)
    pairs = (np.stack((cosine, sine), axis=1), np.stack((-sine, cosine), axis=1))
    return np.stack(pairs, axis=0).astype(np.float32)


def halves(values):
    upper = values.astype(jnp.bfloat16)
    return upper, (values - upper.astype(jnp.float32)).astype(jnp.bfloat16)


def table_halves(table):
    values = table.reshape(2 * table.shape[1], -1)
    upper = values.astype(ml_dtypes.bfloat16)
    lower = (values - upper.astype(np.float32)).astype(ml_dtypes.bfloat16)
    return np.stack((upper, lower))


def dot(first, second):
    return jnp.dot(first, second, preferred_element_type=jnp.float32)


def times_table(values, table):
    upper, lower = halves(values)
    return dot(upper, table[0]) + (dot(upper, table[1]) + dot(lower, table[0]))


def table_times(table, values):
    upper, lower = halves(values)
    return dot(table[0], upper) + (dot(table[1], upper) + dot(table[0], lower))


def meet(group, devices):
    me = lax.axis_index(group)
    barrier = pltpu.get_barrier_semaphore()
    for step in range(1, devices):
        peer = lax.rem(me + step, devices)
        pl.semaphore_signal(
            barrier, inc=1, device_id={group: peer}, device_id_type=pl.DeviceIdType.MESH
        )
    pl.semaphore_wait(barrier, devices - 1)
    return me


def pieces(values, length):
    return [values[:, k * length : (k + 1) * length] for k in range(values.shape[1] // length)]


def transform_x(source, target, table, rows, length):
    def body(group, carry):
        column = []
        for k in range(width):
            picked = pl.ds(width * group + k, length, stride=rows)
            column.append(jnp.concatenate([source[c, picked, :] for c in range(2)], axis=0))
        wave = pieces(table_times(table, jnp.concatenate(column, axis=1)), length)
        for k in range(width):
            picked = pl.ds(width * group + k, length, stride=rows)
            for c in range(2):
                target[c, picked, :] = wave[k][c * length : (c + 1) * length]
        return carry

    lax.fori_loop(0, rows // width, body, 0)


def remote(source, target, sent, got, peer):
    copy = pltpu.make_async_remote_copy(
        src_ref=source, dst_ref=target, send_sem=sent, recv_sem=got,
        device_id={"grid": peer}, device_id_type=pl.DeviceIdType.MESH,
    )
    copy.start()
    return copy


def arrive(grids, resp, orbital, left_x, right_z, left_y, out, away, here, sent, got, own, ready):
    rows, length = orbital.shape[0], orbital.shape[1]
    block, part = rows * rows, rows * rows // 2
    me = lax.axis_index("grid")
    copies = {}
    for harmonic in range(2):
        transform_x(resp.at[harmonic], away.at[harmonic], left_x, rows, length)
        for half in range(2):
            kept = pl.ds(half * part, part)

            def taken(device):
                first = pl.multiple_of(device * block + half * part, part)
                return away.at[harmonic, :, pl.ds(first, part), :]

            mine = pltpu.make_async_copy(
                taken(me), here.at[harmonic, me, :, kept, :], own.at[harmonic, half]
            )
            mine.start()
            steps = []
            for step in range(1, grids):
                peer = lax.rem(me + step, grids)
                steps.append(
                    remote(
                        taken(peer), here.at[harmonic, me, :, kept, :],
                        sent.at[harmonic, half, step], got.at[harmonic, half, step], peer,
                    )
                )
            copies[harmonic, half] = (mine, steps)
    for harmonic in range(2):
        for half in range(2):
            mine, steps = copies[harmonic, half]
            mine.wait()
            for copy in steps:
                copy.wait_recv()

            def transform_zy(group, carry):
                lines = []
                for k in range(width):
                    plane = half * (rows // 2) + width * group + k
                    at = pl.ds(pl.multiple_of(plane * rows, rows), rows)
                    parts = [
                        jnp.concatenate([here[harmonic, s, c, at, :] for s in range(grids)], axis=0)
                        for c in range(2)
                    ]
                    lines.append(jnp.concatenate(parts, axis=1))
                wave = times_table(jnp.concatenate(lines, axis=0), right_z)
                planes = []
                for k in range(width):
                    line = wave[k * length : (k + 1) * length]
                    planes.append(jnp.concatenate(pieces(line, length), axis=0))
                cell = table_times(left_y[harmonic], jnp.concatenate(planes, axis=1))
                cell = pieces(cell, length)
                for k in range(width):
                    plane = half * (rows // 2) + width * group + k
                    for c in range(2):
                        value = cell[k][c * length : (c + 1) * length]
                        if harmonic == 0:
                            out[c, plane] = value
                        else:
                            out[c, plane] = (out[c, plane] + value) * orbital[plane]
                return carry

            lax.fori_loop(0, rows // 2 // width, transform_zy, 0)
            if harmonic == 1:
                ready(half)
    for mine, steps in copies.values():
        for copy in steps:
            copy.wait_send()


def leave(grids, pot, orbital, left_y, right_z, left_x, out, away, here, sent, got, own, need):
    rows, length = orbital.shape[0], orbital.shape[1]
    block, part = rows * rows, rows * rows // 2
    me = lax.axis_index("grid")
    copies = {}
    for half in range(2):
        need(half)
        kept = pl.ds(half * part, part)
        target = pl.ds(pl.multiple_of(me * block + half * part, part), part)
        for harmonic in range(2):

            def transform_yz(group, carry):
                planes = []
                for k in range(width):
                    plane = half * (rows // 2) + width * group + k
                    weight = orbital[plane]
                    planes.append(
                        jnp.concatenate([pot[c, plane] * weight for c in range(2)], axis=0)
                    )
                wave = table_times(left_y[harmonic], jnp.concatenate(planes, axis=1))
                lines = [
                    jnp.concatenate([piece[:length], piece[length:]], axis=1)
                    for piece in pieces(wave, length)
                ]
                wave = times_table(jnp.concatenate(lines, axis=0), right_z)
                for k in range(width):
                    plane = half * (rows // 2) + width * group + k
                    at = pl.ds(pl.multiple_of(plane * rows, rows), rows)
                    for s in range(grids):
                        first = k * length + s * rows
                        for c in range(2):
                            away[harmonic, s, c, at, :] = wave[
                                first : first + rows, c * length : (c + 1) * length
                            ]
                return carry

            lax.fori_loop(0, rows // 2 // width, transform_yz, 0)
            mine = pltpu.make_async_copy(
                away.at[harmonic, me, :, kept, :], here.at[harmonic, :, target, :],
                own.at[harmonic, half],
            )
            mine.start()
            steps = []
            for step in range(1, grids):
                peer = lax.rem(me + step, grids)
                steps.append(
                    remote(
                        away.at[harmonic, peer, :, kept, :], here.at[harmonic, :, target, :],
                        sent.at[harmonic, half, step], got.at[harmonic, half, step], peer,
                    )
                )
            copies[harmonic, half] = (mine, steps)
    for harmonic in range(2):
        for half in range(2):
            mine, steps = copies[harmonic, half]
            mine.wait()
            for copy in steps:
                copy.wait_recv()
        transform_x(here.at[harmonic], out.at[harmonic], left_x, rows, length)
    for mine, steps in copies.values():
        for copy in steps:
            copy.wait_send()


def nothing(half):
    del half


def arrive_kernel(grids, resp, orbital, tables, out, *scratch):
    meet("grid", grids)
    left_y = [tables.at[0], tables.at[1]]
    arrive(grids, resp, orbital, tables.at[0], tables.at[2], left_y, out, *scratch, nothing)


def leave_kernel(grids, pot, orbital, tables, out, *scratch):
    meet("grid", grids)
    left_y = [tables.at[3], tables.at[4]]
    leave(grids, pot, orbital, left_y, tables.at[5], tables.at[3], out, *scratch, nothing)


def basic_tables(length):
    tables = []
    turn = (2, 3, 0, 1)
    flip = np.array([1.0, -1.0], np.float32)
    backward, forward = dft_pair(length, 1.0), dft_pair(length, -1.0)
    tables.append(table_halves(backward.transpose(turn)))
    tables.append(table_halves((backward * flip[:, None]).transpose(turn)))
    tables.append(table_halves(backward))
    tables.append(table_halves(forward.transpose(turn)))
    tables.append(table_halves((forward * flip[:, None, None, None]).transpose(turn)))
    tables.append(table_halves(forward))
    return tables


def whole_kernel(
    grids, resp, orbital, kernel, weights, tables, result, part, got_half, half_sum, got_own, dens,
    away, here, back_away, back_here, out, in_away, in_here, out_away, out_here,
    pair_sent, pair_got, sent, got, in_sent, in_got, in_own, out_sent, out_got, out_own,
):
    devices = 4 * grids
    planes, length = part.shape[1], part.shape[2]
    own = planes // 4
    few = own // 2
    rows = length // devices
    block = 2 * own * rows
    band, grid = lax.axis_index("band"), lax.axis_index("grid")
    me = band * grids + grid

    def at(device):
        return {"band": device // grids, "grid": lax.rem(device, grids)}

    barrier = pltpu.get_barrier_semaphore()

    def greet(step, carry):
        pl.semaphore_signal(
            barrier, inc=1, device_id=at(lax.rem(me + step, devices)),
            device_id_type=pl.DeviceIdType.MESH,
        )
        return carry

    lax.fori_loop(1, devices, greet, 0)
    pl.semaphore_wait(barrier, devices - 1)

    low_bit, high_bit = lax.rem(band, 2), band // 2
    near = {"band": 2 * high_bit + (1 - low_bit), "grid": grid}
    far = {"band": 2 * (1 - high_bit) + low_bit, "grid": grid}

    def pair_copy(source, target, place, *index):
        return pltpu.make_async_remote_copy(
            src_ref=source, dst_ref=target, send_sem=pair_sent.at[index],
            recv_sem=pair_got.at[index], device_id=place, device_id_type=pl.DeviceIdType.MESH,
        )

    def add_bands(half):
        base = half * 2 * own
        kept = pl.ds(half * own, own)
        first = pair_copy(
            part.at[:, pl.ds(base + (1 - low_bit) * own, own)], got_half.at[:, kept], near, 0, half
        )
        first.start()
        first.wait()

        def add_half(plane, carry):
            for c in range(2):
                half_sum[c, half * own + plane] = (
                    part[c, base + low_bit * own + plane] + got_half[c, half * own + plane]
                )
            return carry

        lax.fori_loop(0, own, add_half, 0)
        second = pair_copy(
            half_sum.at[:, pl.ds(half * own + (1 - high_bit) * few, few)],
            got_own.at[:, pl.ds(half * few, few)], far, 1, half,
        )
        second.start()
        second.wait()
        for plane in range(few):
            for c in range(2):
                dens[c, half * few + plane] = (
                    half_sum[c, half * own + high_bit * few + plane]
                    + got_own[c, half * few + plane]
                )

    arrive(
        grids, resp, orbital, tables.at[0], tables.at[2], [tables.at[0], tables.at[1]], part,
        in_away, in_here, in_sent, in_got, in_own, add_bands,
    )

    def exchange(source, target, index):
        mine = pl.ds(pl.multiple_of(me * block, block), block)

        def copy_of(step):
            peer = lax.rem(me + step, devices)
            return pltpu.make_async_remote_copy(
                src_ref=source.at[pl.ds(pl.multiple_of(peer * block, block), block)],
                dst_ref=target.at[mine],
                send_sem=sent.at[index, step],
                recv_sem=got.at[index, step],
                device_id=at(peer),
                device_id_type=pl.DeviceIdType.MESH,
            )

        def start(step, carry):
            copy_of(step).start()
            return carry

        def finish(step, carry):
            copy_of(step).wait()
            return carry

        lax.fori_loop(1, devices, start, 0)
        target[mine, :] = source[mine, :]
        lax.fori_loop(1, devices, finish, 0)

    def lane(values, index):
        return values[:, index * length : (index + 1) * length]

    def beside(values):
        lines = [
            jnp.concatenate([lane(values, p)[:length], lane(values, p)[length:]], axis=1)
            for p in range(own)
        ]
        return jnp.concatenate(lines, axis=0)

    def spread(c, plane, row):
        return pl.ds((c * own + plane) * rows + row, devices, stride=block)

    field = jnp.concatenate(
        [jnp.concatenate([dens[c, p] for c in range(2)], axis=0) for p in range(own)], axis=1
    )
    wave = times_table(beside(table_times(tables.at[6], field)), tables.at[5])
    for p in range(own):
        for row in range(rows):
            top = p * length + row * devices
            for c in range(2):
                away[spread(c, p, row), :] = lane(wave[top : top + devices], c)
    exchange(away, here, 0)
    field = jnp.concatenate(
        [
            jnp.concatenate(
                [here[spread(c, p, row), :] for c in range(2) for p in range(own)], axis=0
            )
            for row in range(rows)
        ],
        axis=1,
    )
    wave = table_times(tables.at[7], field)
    weight = weights[...]
    wave = jnp.concatenate([wave[:length] * weight, wave[length:] * weight], axis=0)
    field = table_times(tables.at[8], wave)
    for row in range(rows):
        for c in range(2):
            for p in range(own):
                top = (c * own + p) * devices
                back_away[spread(c, p, row), :] = lane(field[top : top + devices], row)
    exchange(back_away, back_here, 1)
    wave = jnp.concatenate(
        [
            jnp.concatenate(
                [back_here[spread(c, p, row), :] for c in range(2) for row in range(rows)], axis=0
            )
            for p in range(own)
        ],
        axis=1,
    )
    cell = times_table(beside(table_times(tables.at[9], wave)), tables.at[2])
    third = []
    for half in range(2):
        low = half * 2 * own + low_bit * own + high_bit * few
        for q in range(few):
            p = half * few + q
            for c in range(2):
                value = lane(cell[p * length : (p + 1) * length], c)
                out[c, low + q] = value + kernel[low + q] * dens[c, p]
        mine = out.at[:, pl.ds(low, few)]
        third.append(pair_copy(mine, mine, far, 2, half))
        third[half].start()

    def gather(half):
        third[half].wait()
        mine = out.at[:, pl.ds(half * 2 * own + low_bit * own, own)]
        fourth = pair_copy(mine, mine, near, 3, half)
        fourth.start()
        fourth.wait()

    leave(
        grids, out, orbital, [tables.at[3], tables.at[4]], tables.at[5], tables.at[3], result,
        out_away, out_here, out_sent, out_got, out_own, gather,
    )


def whole(grids, response, orbital, kernel_xc):
    planes, length = orbital.shape[0], orbital.shape[1]
    devices = 4 * grids
    own, rows = planes // 4, length // devices
    few = own // 2
    turn = (2, 3, 0, 1)
    kept = np.arange(rows)[:, None] + rows * np.arange(devices)[None, :]
    kept = kept.reshape(-1)
    place = np.array([0, 2, 1, 3])
    plane = np.arange(own)
    numbers = (
        (plane // few * 2 * own + plane % few)[:, None, None]
        + few * place[None, :, None]
        + planes * np.arange(grids)[None, None, :]
    ).reshape(-1)
    mine = (lax.axis_index("band") * grids + lax.axis_index("grid")) * rows
    freqs = signed_freq(jnp.arange(length, dtype=jnp.int32), length)
    own_freqs = signed_freq(mine + jnp.arange(rows, dtype=jnp.int32), length)
    weights = coulomb(freqs, own_freqs, freqs, length).reshape(length, rows * length)
    tables = basic_tables(length) + [
        table_halves(dft_pair(length, -1.0, columns=kept).transpose(turn)),
        table_halves(dft_pair(length, -1.0, rows=numbers).transpose(turn)),
        table_halves(dft_pair(length, 1.0, columns=numbers).transpose(turn)),
        table_halves(dft_pair(length, 1.0, rows=kept).transpose(turn)),
    ]
    operands = (response, orbital, kernel_xc, weights, np.stack(tables))

    def space(*shape):
        return pltpu.VMEM(shape, jnp.float32)

    parts = space(2 * own * length, length)
    flat = space(2, 2, length * planes, length)
    blocks = space(2, grids, 2, planes * planes, length)
    wide = space(2, planes, length, length)
    meets = pltpu.SemaphoreType.DMA((2, 2, grids))
    return pl.pallas_call(
        functools.partial(whole_kernel, grids),
        out_shape=jax.ShapeDtypeStruct(response.shape, jnp.float32),
        in_specs=[pl.BlockSpec(memory_space=pltpu.VMEM)] * len(operands),
        out_specs=pl.BlockSpec(memory_space=pltpu.VMEM),
        scratch_shapes=[
            wide,
            space(2, 2 * own, length, length),
            space(2, 2 * own, length, length),
            space(2, own, length, length),
            space(2, own, length, length),
            parts, parts, parts, parts,
            wide,
            flat, blocks, blocks, flat,
            pltpu.SemaphoreType.DMA((4, 2)),
            pltpu.SemaphoreType.DMA((4, 2)),
            pltpu.SemaphoreType.DMA((2, devices)),
            pltpu.SemaphoreType.DMA((2, devices)),
            meets, meets, pltpu.SemaphoreType.DMA((2, 2)),
            meets, meets, pltpu.SemaphoreType.DMA((2, 2)),
        ],
        compiler_params=pltpu.CompilerParams(
            collective_id=2, has_side_effects=True, vmem_limit_bytes=56 * 2**20
        ),
    )(*operands)


def call(kernel, grids, rows, length, out_shape, by_source, collective_id, *operands):
    flat = (2, 2, length * rows, length)
    blocks = (2, grids, 2, rows * rows, length)
    return pl.pallas_call(
        functools.partial(kernel, grids),
        out_shape=jax.ShapeDtypeStruct(out_shape, jnp.float32),
        in_specs=[pl.BlockSpec(memory_space=pltpu.VMEM)] * len(operands),
        out_specs=pl.BlockSpec(memory_space=pltpu.VMEM),
        scratch_shapes=[
            pltpu.VMEM(flat if by_source else blocks, jnp.float32),
            pltpu.VMEM(blocks if by_source else flat, jnp.float32),
            pltpu.SemaphoreType.DMA((2, 2, grids)),
            pltpu.SemaphoreType.DMA((2, 2, grids)),
            pltpu.SemaphoreType.DMA((2, 2)),
        ],
        compiler_params=pltpu.CompilerParams(
            collective_id=collective_id, has_side_effects=True, vmem_limit_bytes=40 * 2**20
        ),
    )(*operands)


def ein(form, operand, table):
    return jnp.einsum(form, operand, table, precision=high)


def signed_freq(positions, length):
    return jnp.where(positions < (length + 1) // 2, positions, positions - length).astype(
        jnp.float32
    )


def coulomb(freq_first, freq_second, freq_third, length):
    squares = (
        freq_first[:, None, None] ** 2
        + freq_second[None, :, None] ** 2
        + freq_third[None, None, :] ** 2
    )
    edge_len = spacing * length
    return jnp.where(
        squares > 0.5, edge_len * edge_len / (math.pi * jnp.maximum(squares, 1.0)), 0.0
    )


def hartree(density, axes, device, devices, numbers):
    length = density.shape[-1]
    forward, backward = dft_pair(length, -1.0), dft_pair(length, 1.0)
    wave = ein("cxyz,cydk->dxkz", density, forward)
    wave = ein("dxkz,dzem->exkm", wave, forward)
    wave = lax.all_to_all(wave, axes, split_axis=2, concat_axis=1, tiled=True)
    rows = length // devices
    mine = device * rows + jnp.arange(rows, dtype=jnp.int32)
    freqs = signed_freq(jnp.arange(length, dtype=jnp.int32), length)
    weights = coulomb(freqs, signed_freq(mine, length), freqs, length)
    wave = ein("cxyz,cxdk->dkyz", wave, dft_pair(length, -1.0, rows=numbers)) * weights
    wave = ein("dkyz,dkex->exyz", wave, dft_pair(length, 1.0, columns=numbers))
    wave = lax.all_to_all(wave, axes, split_axis=1, concat_axis=2, tiled=True)
    cell = ein("dxkz,dzem->exkm", wave, backward)
    return ein("cxyz,cydk->dxkz", cell, backward)


def on_device(bands, grids, ground, response, kernel_xc):
    grid_len = ground.shape[2]
    planes = ground.shape[1]
    orbital = ground[0]
    flat = response.reshape(2, 2, grid_len * planes, grid_len)
    if bands == 4 and planes % 8 == 0 and grid_len % (4 * grids) == 0:
        out = whole(grids, flat, orbital, kernel_xc)
    else:
        tables = np.stack(basic_tables(grid_len))
        partial = call(
            arrive_kernel, grids, planes, grid_len, (2, planes, grid_len, grid_len), True, 0,
            flat, orbital, tables,
        )
        dens = lax.psum(partial, "band")
        pot = hartree(dens, "grid", lax.axis_index("grid"), grids, None) + kernel_xc * dens
        out = call(
            leave_kernel, grids, planes, grid_len, (2, 2, grid_len * planes, grid_len), False, 1,
            pot, orbital, tables,
        )
    return out.reshape(1, 2, 2, grid_len, planes, grid_len)


def solution(mesh):
    bands, grids = mesh.shape["band"], mesh.shape["grid"]

    def body(ground, response, kernel_xc):
        return on_device(bands, grids, ground, response, kernel_xc)

    return jax.shard_map(
        body,
        mesh=mesh,
        in_specs=(
            P("band", "grid", None, None),
            P("band", None, None, None, "grid", None),
            P("grid", None, None),
        ),
        out_specs=P("band", None, None, None, "grid", None),
        check_vma=False,
    )
```

time: 281 us -> 260 us (0.925)
  Pallas kernels: 272 us -> 254 us
  local copies, waits for them, and re-layouts: 8.61 us -> 4.77 us
    pallas_call x3 -> x1, Pallas kernels: 272 us -> 254 us  [whole(): pl.pallas_call(functools.partial(whole_kernel, grids), out_shape=jax.Shap...]
    unnamed x29 -> x1, local copies, waits for them, and re-layouts: 8.41 us -> 4.57 us
where the time goes in v4:
time: 260 us; the launch traced here: 259 us
  Pallas kernels  254 us (98%)
  local copies, waits for them, and re-layouts  4.77 us (2%)
    pallas_call x1, Pallas kernels, whole(): pl.pallas_call(functools.partial(whole_kernel, grids), out_shape=jax.Shap...  254 us

profile of v4, /device:TPU:10, one launch (start us, length us, event | category | flops | bytes accessed | tf_op | source)
XLA Modules:
  0.0 259.4 jit_solution(18182203465008579837)
XLA Ops:
  0.0 0.1 broadcast_add_fusion
  0.1 0.2 add.71
  0.3 0.8 divide_select_fusion.weights
  1.1 253.7 %shard_map.46 = f32[2,2,2048,128]{3,2,1,0:T(8,128)} custom-call(f32[2,2,2048,128]{3,2,1,0:T(8,128)} %bitcast.11, f32[16,128,128]{2,1,0:T(8,128)} %bitcast.12, f32[16,128,128]{2,1,0:T(8,128)} %kernel.1, f32[128,512]{1,0:T(8,128)} %divide_select_fusion.weights, bf16[10,2,256,256]{3,2,1,0:T(8,128)(2,1)} %constant.32.clone.tables), custom_call_target="tpu_custom_call" | custom-call | tf_op jit(solution)/shard_map/pallas_call | solution.py:471
  254.8 4.6 %copy.10 = f32[1,2,2,128,16,128]{5,4,3,2,1,0:T(8,128)} copy(f32[1,2,2,128,16,128]{5,4,3,2,1,0:T(8,128)} %bitcast.10) | data formatting | bytes 8388608
  (3 shorter events, 0.0 us)

commit v5 on v4

--- a/solution.py
+++ b/solution.py
@@ -83,6 +83,10 @@
     lax.fori_loop(0, rows // width, body, 0)
 
 
+def far_first(devices):
+    return sorted(range(1, devices), key=lambda step: abs(2 * step - devices))
+
+
 def remote(source, target, sent, got, peer):
     copy = pltpu.make_async_remote_copy(
         src_ref=source, dst_ref=target, send_sem=sent, recv_sem=got,
@@ -92,12 +96,13 @@
     return copy
 
 
-def arrive(grids, resp, orbital, left_x, right_z, left_y, out, away, here, sent, got, own, ready):
+def arrive(grids, resp, orbital, left_x, right_z, left_y, out, away, here, sent, got, own, ready, before):
     rows, length = orbital.shape[0], orbital.shape[1]
     block, part = rows * rows, rows * rows // 2
     me = lax.axis_index("grid")
     copies = {}
     for harmonic in range(2):
+        before(harmonic)
         transform_x(resp.at[harmonic], away.at[harmonic], left_x, rows, length)
         for half in range(2):
             kept = pl.ds(half * part, part)
@@ -111,7 +116,7 @@
             )
             mine.start()
             steps = []
-            for step in range(1, grids):
+            for step in far_first(grids):
                 peer = lax.rem(me + step, grids)
                 steps.append(
                     remote(
@@ -120,6 +125,7 @@
                     )
                 )
             copies[harmonic, half] = (mine, steps)
+    before(2)
     for harmonic in range(2):
         for half in range(2):
             mine, steps = copies[harmonic, half]
@@ -162,7 +168,7 @@
             copy.wait_send()
 
 
-def leave(grids, pot, orbital, left_y, right_z, left_x, out, away, here, sent, got, own, need):
+def leave(grids, pot, orbital, left_y, right_z, left_x, out, away, here, sent, got, own, need, done):
     rows, length = orbital.shape[0], orbital.shape[1]
     block, part = rows * rows, rows * rows // 2
     me = lax.axis_index("grid")
@@ -205,7 +211,7 @@
             )
             mine.start()
             steps = []
-            for step in range(1, grids):
+            for step in far_first(grids):
                 peer = lax.rem(me + step, grids)
                 steps.append(
                     remote(
@@ -221,6 +227,7 @@
             for copy in steps:
                 copy.wait_recv()
         transform_x(here.at[harmonic], out.at[harmonic], left_x, rows, length)
+        done(harmonic)
     for mine, steps in copies.values():
         for copy in steps:
             copy.wait_send()
@@ -233,13 +240,13 @@
 def arrive_kernel(grids, resp, orbital, tables, out, *scratch):
     meet("grid", grids)
     left_y = [tables.at[0], tables.at[1]]
-    arrive(grids, resp, orbital, tables.at[0], tables.at[2], left_y, out, *scratch, nothing)
+    arrive(grids, resp, orbital, tables.at[0], tables.at[2], left_y, out, *scratch, nothing, nothing)
 
 
 def leave_kernel(grids, pot, orbital, tables, out, *scratch):
     meet("grid", grids)
     left_y = [tables.at[3], tables.at[4]]
-    leave(grids, pot, orbital, left_y, tables.at[5], tables.at[3], out, *scratch, nothing)
+    leave(grids, pot, orbital, left_y, tables.at[5], tables.at[3], out, *scratch, nothing, nothing)
 
 
 def basic_tables(length):
@@ -257,7 +264,8 @@
 
 
 def whole_kernel(
-    grids, resp, orbital, kernel, weights, tables, result, part, got_half, half_sum, got_own, dens,
+    grids, resp_far, orbital_far, kernel_far, tables_far, weights, result_far, resp, orbital,
+    kernel, tables, result, moved, part, got_half, half_sum, got_own, dens,
     away, here, back_away, back_here, out, in_away, in_here, out_away, out_here,
     pair_sent, pair_got, sent, got, in_sent, in_got, in_own, out_sent, out_got, out_own,
 ):
@@ -269,6 +277,30 @@
     block = 2 * own * rows
     band, grid = lax.axis_index("band"), lax.axis_index("grid")
     me = band * grids + grid
+
+    def load(source, target, index):
+        copy = pltpu.make_async_copy(source, target, moved.at[index])
+        copy.start()
+        return copy
+
+    count = tables.shape[0]
+    loads = [
+        load(tables_far.at[pl.ds(0, 1)], tables.at[pl.ds(0, 1)], 0),
+        load(resp_far.at[0], resp.at[0], 1),
+        load(resp_far.at[1], resp.at[1], 2),
+        load(tables_far.at[pl.ds(1, count - 1)], tables.at[pl.ds(1, count - 1)], 3),
+        load(orbital_far, orbital, 4),
+        load(kernel_far, kernel, 5),
+    ]
+
+    def before(stage):
+        for copy in (loads[:2], loads[2:3], loads[3:])[stage]:
+            copy.wait()
+
+    stores = []
+
+    def done(harmonic):
+        stores.append(load(result.at[harmonic], result_far.at[harmonic], 6 + harmonic))
 
     def at(device):
         return {"band": device // grids, "grid": lax.rem(device, grids)}
@@ -327,7 +359,7 @@
 
     arrive(
         grids, resp, orbital, tables.at[0], tables.at[2], [tables.at[0], tables.at[1]], part,
-        in_away, in_here, in_sent, in_got, in_own, add_bands,
+        in_away, in_here, in_sent, in_got, in_own, add_bands, before,
     )
 
     def exchange(source, target, index):
@@ -429,8 +461,10 @@
 
     leave(
         grids, out, orbital, [tables.at[3], tables.at[4]], tables.at[5], tables.at[3], result,
-        out_away, out_here, out_sent, out_got, out_own, gather,
-    )
+        out_away, out_here, out_sent, out_got, out_own, gather, done,
+    )
+    for copy in stores:
+        copy.wait()
 
 
 def whole(grids, response, orbital, kernel_xc):
@@ -458,7 +492,7 @@
         table_halves(dft_pair(length, 1.0, columns=numbers).transpose(turn)),
         table_halves(dft_pair(length, 1.0, rows=kept).transpose(turn)),
     ]
-    operands = (response, orbital, kernel_xc, weights, np.stack(tables))
+    operands = (response, orbital, kernel_xc, np.stack(tables), weights)
 
     def space(*shape):
         return pltpu.VMEM(shape, jnp.float32)
@@ -471,9 +505,16 @@
     return pl.pallas_call(
         functools.partial(whole_kernel, grids),
         out_shape=jax.ShapeDtypeStruct(response.shape, jnp.float32),
-        in_specs=[pl.BlockSpec(memory_space=pltpu.VMEM)] * len(operands),
-        out_specs=pl.BlockSpec(memory_space=pltpu.VMEM),
+        in_specs=[pl.BlockSpec(memory_space=pl.ANY)] * 4
+        + [pl.BlockSpec(memory_space=pltpu.VMEM)],
+        out_specs=pl.BlockSpec(memory_space=pl.ANY),
         scratch_shapes=[
+            flat,
+            space(planes, length, length),
+            space(planes, length, length),
+            pltpu.VMEM((len(tables), 2, 2 * length, 2 * length), jnp.bfloat16),
+            flat,
+            pltpu.SemaphoreType.DMA((8,)),
             wide,
             space(2, 2 * own, length, length),
             space(2, 2 * own, length, length),

time: 260 us -> 254 us (0.977)
  Pallas kernels: 254 us -> 247 us
    pallas_call x1, Pallas kernels: 254 us -> 247 us  [whole(): pl.pallas_call(functools.partial(whole_kernel, grids), out_shape=jax.Shap...]
where the time goes in v5:
time: 254 us; the launch traced here: 253 us
  Pallas kernels  247 us (97%)
  local copies, waits for them, and re-layouts  4.77 us (2%)
    pallas_call x1, Pallas kernels, whole(): pl.pallas_call(functools.partial(whole_kernel, grids), out_shape=jax.Shap...  247 us

profile of v5, /device:TPU:10, one launch (start us, length us, event | category | flops | bytes accessed | tf_op | source)
XLA Modules:
  0.0 252.9 jit_solution(6616819326297290429)
XLA Ops:
  0.0 0.1 broadcast_add_fusion
  0.1 0.2 add.71
  0.3 0.8 divide_select_fusion.weights
  1.1 247.2 %shard_map.46 = f32[2,2,2048,128]{3,2,1,0:T(8,128)} custom-call(f32[2,2,2048,128]{3,2,1,0:T(8,128)} %bitcast.11, f32[16,128,128]{2,1,0:T(8,128)} %bitcast.12, f32[16,128,128]{2,1,0:T(8,128)} %kernel_far.1, bf16[10,2,256,256]{3,2,1,0:T(8,128)(2,1)} %constant.32.clone.tables_far, f32[128,512]{1,0:T(8,128)} %divide_select_fusion.weights), custom_call_target="tpu_custom_call" | custom-call | tf_op jit(solution)/shard_map/pallas_call | solution.py:505
  248.3 4.6 %copy.10 = f32[1,2,2,128,16,128]{5,4,3,2,1,0:T(8,128)} copy(f32[1,2,2,128,16,128]{5,4,3,2,1,0:T(8,128)} %bitcast.10) | data formatting | bytes 8388608
  (3 shorter events, 0.0 us)

commit v6 on v5

--- a/solution.py
+++ b/solution.py
@@ -43,12 +43,16 @@
 
 def times_table(values, table):
     upper, lower = halves(values)
-    return dot(upper, table[0]) + (dot(upper, table[1]) + dot(lower, table[0]))
+    count = values.shape[0]
+    both = dot(jnp.concatenate((upper, lower), axis=0), table[0])
+    return both[:count] + (dot(upper, table[1]) + both[count:])
 
 
 def table_times(table, values):
     upper, lower = halves(values)
-    return dot(table[0], upper) + (dot(table[1], upper) + dot(table[0], lower))
+    count = table.shape[1]
+    both = dot(jnp.concatenate((table[0], table[1]), axis=0), upper)
+    return both[:count] + (both[count:] + dot(table[0], lower))
 
 
 def meet(group, devices):

time: 254 us -> 254 us (level)
  no operation moved by 1% of the time
where the time goes in v6:
time: 254 us; the launch traced here: 253 us
  Pallas kernels  247 us (97%)
  local copies, waits for them, and re-layouts  4.77 us (2%)
    pallas_call x1, Pallas kernels, whole(): pl.pallas_call(functools.partial(whole_kernel, grids), out_shape=jax.Shap...  247 us

profile of v6, /device:TPU:10, one launch (start us, length us, event | category | flops | bytes accessed | tf_op | source)
XLA Modules:
  0.0 252.8 jit_solution(18318165542151249056)
XLA Ops:
  0.0 0.1 broadcast_add_fusion
  0.1 0.2 add.71
  0.3 0.8 divide_select_fusion.weights
  1.1 247.1 %shard_map.46 = f32[2,2,2048,128]{3,2,1,0:T(8,128)} custom-call(f32[2,2,2048,128]{3,2,1,0:T(8,128)} %bitcast.11, f32[16,128,128]{2,1,0:T(8,128)} %bitcast.12, f32[16,128,128]{2,1,0:T(8,128)} %kernel_far.1, bf16[10,2,256,256]{3,2,1,0:T(8,128)(2,1)} %constant.32.clone.tables_far, f32[128,512]{1,0:T(8,128)} %divide_select_fusion.weights), custom_call_target="tpu_custom_call" | custom-call | tf_op jit(solution)/shard_map/pallas_call | solution.py:509
  248.2 4.6 %copy.10 = f32[1,2,2,128,16,128]{5,4,3,2,1,0:T(8,128)} copy(f32[1,2,2,128,16,128]{5,4,3,2,1,0:T(8,128)} %bitcast.10) | data formatting | bytes 8388608
  (3 shorter events, 0.0 us)
